TPU v7x, 128 devices: a whole 4x4x4 slice. The times are simulated.
128 devices in a mesh: dp: 4 (over x), ep: 16 (over y_lo, z, core), tp: 2 (over y_hi).
Axes of the slice: x: 4, y: 4 (y_hi: 2, y_lo: 2; y = y_hi * 2 + y_lo), z: 4, core: 2. Of those that a mesh axis runs over, the one named last changes fastest.
Arguments:
- tokens: bfloat16 [8192, 1280], P(('dp', 'ep')), may hold values from -6 to 6
- grad_out: bfloat16 [8192, 1280], P(('dp', 'ep')), may hold values from -6 to 6
- doc_ids: int32 [4, 2048], P('dp'), may hold values from 0 to 1, never falling along the last dimension, each value on 1 to 1280 neighbouring positions
- piece_starts: int32 [4, 2], P('dp'), may hold values from 0 to 1792, as said below
- piece_ends: int32 [4, 2], P('dp'), may hold values from 256 to 2048, as said below
- routes: int32 [8192, 7], P(('dp', 'ep')), may hold values from 0 to 62, all different within a row; in each aligned block of 128 rows (0 to 127, 128 to 255, ...) at most 16 rows name the same one
- norm1_gain: float32 [1280], replicated, may hold values from 0.5 to 1.5
- norm2_gain: float32 [1280], replicated, may hold values from 0.5 to 1.5
- query_weight: bfloat16 [1280, 1280], P(None, 'tp'), may hold values from -0.15625 to 0.15625
- key_weight: bfloat16 [1280, 1280], P(None, 'tp'), may hold values from -0.15625 to 0.15625
- value_weight: bfloat16 [1280, 1280], P(None, 'tp'), may hold values from -0.15625 to 0.15625
- output_weight: bfloat16 [1280, 1280], P('tp'), may hold values from -1.5 to 1.5
- router_weight: bfloat16 [1280, 63], replicated, may hold values from -0.079589844 to 0.079589844
- shared_gate: bfloat16 [1280, 896], P(None, 'tp'), may hold values from -0.15625 to 0.15625
- shared_up: bfloat16 [1280, 896], P(None, 'tp'), may hold values from -0.15625 to 0.15625
- shared_down: bfloat16 [896, 1280], P('tp'), may hold values from -0.375 to 0.375
- expert_gate: bfloat16 [64, 1280, 896], P('ep', None, 'tp'), may hold values from -0.15625 to 0.15625
- expert_up: bfloat16 [64, 1280, 896], P('ep', None, 'tp'), may hold values from -0.15625 to 0.15625
- expert_down: bfloat16 [64, 896, 1280], P('ep', 'tp'), may hold values from -0.75 to 0.75
Outputs:
- output: bfloat16 [8192, 1280], P(('dp', 'ep'))
- grad_tokens: float32 [8192, 1280], P(('dp', 'ep'))
- grad_norm1_gain: float32 [1280], P(('dp', 'ep'))
- grad_norm2_gain: float32 [1280], P(('dp', 'ep'))
- grad_query_weight: float32 [1280, 1280], P(('dp', 'ep'), 'tp')
- grad_key_weight: float32 [1280, 1280], P(('dp', 'ep'), 'tp')
- grad_value_weight: float32 [1280, 1280], P(('dp', 'ep'), 'tp')
- grad_output_weight: float32 [1280, 1280], P('tp', ('dp', 'ep'))
- grad_router_weight: float32 [1280, 63], P(('dp', 'ep'))
- grad_shared_gate: float32 [1280, 896], P(('dp', 'ep'), 'tp')
- grad_shared_up: float32 [1280, 896], P(('dp', 'ep'), 'tp')
- grad_shared_down: float32 [896, 1280], P('tp', ('dp', 'ep'))
- grad_expert_gate: float32 [64, 1280, 896], P('ep', 'dp', 'tp')
- grad_expert_up: float32 [64, 1280, 896], P('ep', 'dp', 'tp')
- grad_expert_down: float32 [64, 896, 1280], P('ep', 'tp', 'dp')
Inputs may be any that keep to these rules, and one draw needn't show every extreme that they name: `doc_ids`: document numbers never fall along a row; a document has at most 1280 tokens. `piece_starts`: piece k of a row starts at k * 1024 or at k * 1024 + 768. `piece_ends`: each end is its piece's start plus 256. `routes`: A token names 7 different experts; within the tokens of one device no expert is named more than 16 times.
All inputs are finite; a program needn't handle non-finite values.
Results may differ from a plain program's by a relative error of at most 0.02.
Values may be sent and summed in bfloat16 or wider, within the bound.
No kernel may reach another device: no remote copies, remote signals or barrier semaphores. Data moves between devices by JAX's collectives and lax.ppermute only.
A program may use at most 320 MiB of HBM per device.

v0:
```python
import jax
import jax.numpy as jnp
from jax import lax
from jax.sharding import PartitionSpec as P

HEAD_DIM = 128
TOPK = 7


EPSILON = 1e-06
NEG_FILL = -1e30
BASE = 10000.0


def side_by_side(arrays, axis, dim, along):
    ends, at = ([], 0)
    for a in arrays[:-1]:
        at += a.shape[along]
        ends.append(at)
    both = jnp.concatenate(arrays, axis=along)
    return tuple(jnp.split(lax.all_gather(both, axis, axis=dim, tiled=True), ends, axis=along))


def from_everyone(value, axis):
    copies = jnp.broadcast_to(value, (lax.axis_size(axis), *value.shape))
    return lax.all_to_all(copies, axis, split_axis=0, concat_axis=0, tiled=True)


def over_copies(value, axis):
    everything = from_everyone(value, axis)
    return jnp.sum(everything, axis=0)


def of_everyone(value, axis):
    return from_everyone(value, axis).astype(jnp.float32).sum(axis=0)


def in_one(arrays, axis):
    ends = [0]
    for a in arrays:
        ends.append(ends[-1] + a.size)
    running = over_copies(jnp.concatenate([a.ravel() for a in arrays]), axis)
    return tuple((running[b:e].reshape(a.shape) for a, b, e in zip(arrays, ends, ends[1:])))


def sent_together(arrays, axis, dim, along):
    both = jnp.concatenate(arrays, axis=along)
    out, at, gathered = (lax.psum_scatter(both, axis, scatter_dimension=dim, tiled=True), 0, [])
    for a in arrays:
        gathered.append(lax.slice_in_dim(out, at, at + a.shape[along], axis=along))
        at += a.shape[along]
    return tuple(gathered)


def split_up(value, dim, size):
    before, after = (value.shape[:dim], value.shape[dim + 1 :])
    return jnp.moveaxis(value.reshape(*before, size, -1, *after), dim, 0)


def sum_packed(arrays, axis, dims):
    size = lax.axis_size(axis)
    blocks = [split_up(a, dim, size) for a, dim in zip(arrays, dims)]
    lines = jnp.concatenate([b.reshape(size, -1) for b in blocks], axis=1)
    width = max(16, -(-lines.shape[1] // 1024) * 8)
    lines = jnp.pad(lines, ((0, 0), (0, width * 128 - lines.shape[1]))).reshape(-1, 128)
    flat, at, gathered = (lax.psum_scatter(lines, axis, tiled=True).reshape(-1), 0, [])
    for b in blocks:
        part = b[0]
        gathered.append(flat[at : at + part.size].reshape(part.shape))
        at += part.size
    return tuple(gathered)


def rotation_tables(positions, width):
    half = width // 2
    frequency = BASE ** (-(jnp.arange(half, dtype=jnp.float32) * 2.0) / width)
    angles = positions.astype(jnp.float32)[:, None] * frequency[None, :]
    return (jnp.cos(angles)[:, None, :], jnp.sin(angles)[:, None, :])


def rotate(values, cosine, sine):
    half = values.shape[-1] // 2
    first = values[..., :half]
    second = values[..., half:]
    return jnp.concatenate(
        [first * cosine - second * sine, first * sine + second * cosine], axis=-1
    )


def attention_mask(query_pos, key_pos, query_doc, key_doc, starts, ends):
    same_doc = query_doc[:, None] == key_doc[None, :]
    causal = key_pos[None, :] <= query_pos[:, None]
    query_in = (
        (query_pos[:, None] >= starts[None, :]) & (query_pos[:, None] < ends[None, :])
    ).astype(jnp.float32)
    key_in = ((key_pos[:, None] >= starts[None, :]) & (key_pos[:, None] < ends[None, :])).astype(
        jnp.float32
    )
    together = jnp.dot(query_in, key_in.T, preferred_element_type=jnp.float32) > 0.5
    return same_doc & (causal | together)


def gated_grads(gate_pre, up_pre, hidden_grad):
    sigmoid = jax.nn.sigmoid(gate_pre)
    activated = gate_pre * sigmoid
    slope = sigmoid * (1.0 + gate_pre * (1.0 - sigmoid))
    return (
        (hidden_grad * up_pre * slope).astype(jnp.bfloat16),
        (hidden_grad * activated).astype(jnp.bfloat16),
    )


def norm_back(unit, inverse, gain, grad):
    gain_grad = jnp.sum(grad * unit, axis=0)
    scaled = grad * gain
    return (gain_grad, inverse * (scaled - unit * jnp.mean(scaled * unit, axis=1, keepdims=True)))


def to_experts(buffer):
    return lax.all_to_all(buffer, "ep", split_axis=0, concat_axis=1, tiled=True)


def from_experts(buffer):
    return lax.all_to_all(buffer, "ep", split_axis=1, concat_axis=0, tiled=True)


def local(
    tokens,
    grad_out,
    doc_ids,
    piece_starts,
    piece_ends,
    routes,
    norm1_gain,
    norm2_gain,
    query_weight,
    key_weight,
    value_weight,
    output_weight,
    router_weight,
    shared_gate,
    shared_up,
    shared_down,
    expert_gate,
    expert_up,
    expert_down,
):
    token_rows = tokens.shape[0]
    width = tokens.shape[1]
    capacity = token_rows // 8
    ep_size = lax.axis_size("ep")
    ep_rank = lax.axis_index("ep")
    group_len = token_rows * ep_size
    local_heads = query_weight.shape[1] // HEAD_DIM
    slot_count = expert_gate.shape[0] * ep_size
    scale = HEAD_DIM ** (-0.5)
    inputs = tokens.astype(jnp.float32)
    first_inverse = lax.rsqrt(jnp.mean(inputs * inputs, axis=1, keepdims=True) + EPSILON)
    first_unit = inputs * first_inverse
    first_normed = (first_unit * norm1_gain).astype(jnp.bfloat16)
    own_pos = ep_rank * token_rows + jnp.arange(token_rows, dtype=jnp.int32)
    key_pos = jnp.arange(group_len, dtype=jnp.int32)
    cosine, sine = rotation_tables(own_pos, HEAD_DIM)
    query_pre = jnp.dot(first_normed, query_weight, preferred_element_type=jnp.float32)
    key_pre = jnp.dot(first_normed, key_weight, preferred_element_type=jnp.float32)
    query_heads = rotate(query_pre.reshape(token_rows, local_heads, HEAD_DIM), cosine, sine).astype(
        jnp.bfloat16
    )
    own_keys = rotate(key_pre.reshape(token_rows, local_heads, HEAD_DIM), cosine, sine).astype(
        jnp.bfloat16
    )
    keys = own_keys.reshape(token_rows, local_heads * HEAD_DIM)
    values = jnp.dot(first_normed, value_weight, preferred_element_type=jnp.float32).astype(
        jnp.bfloat16
    )
    all_keys, all_values = side_by_side((keys, values), "ep", 0, 1)
    key_heads = all_keys.reshape(group_len, local_heads, HEAD_DIM)
    value_heads = all_values.reshape(group_len, local_heads, HEAD_DIM)
    key_doc = doc_ids[0]
    query_doc = lax.dynamic_slice_in_dim(key_doc, ep_rank * token_rows, token_rows)
    visible = attention_mask(own_pos, key_pos, query_doc, key_doc, piece_starts[0], piece_ends[0])
    attended = []
    highest_list = []
    total_list = []
    for head in range(local_heads):
        scores = (
            jnp.einsum(
                "qd,kd->qk",
                query_heads[:, head],
                key_heads[:, head],
                preferred_element_type=jnp.float32,
            )
            * scale
        )
        masked = jnp.where(visible, scores, NEG_FILL)
        highest = jnp.max(masked, axis=1, keepdims=True)
        exponent = jnp.exp(masked - highest)
        total = jnp.sum(exponent, axis=1, keepdims=True)
        weights = (exponent / total).astype(jnp.bfloat16)
        attended.append(
            jnp.dot(weights, value_heads[:, head], preferred_element_type=jnp.float32).astype(
                jnp.bfloat16
            )
        )
        highest_list.append(highest)
        total_list.append(total)
    attended = jnp.concatenate(attended, axis=1)
    attention = over_copies(
        jnp.dot(attended, output_weight, preferred_element_type=jnp.float32), "tp"
    )
    residual = inputs + attention
    second_inverse = lax.rsqrt(jnp.mean(residual * residual, axis=1, keepdims=True) + EPSILON)
    second_unit = residual * second_inverse
    second_normed = (second_unit * norm2_gain).astype(jnp.bfloat16)
    logits = jnp.dot(second_normed, router_weight, preferred_element_type=jnp.float32)
    expert_ids = jnp.arange(router_weight.shape[1], dtype=jnp.int32)
    route_hot = (routes[:, :, None] == expert_ids[None, None, :]).astype(jnp.float32)
    gates = jax.nn.softmax(jnp.sum(route_hot * logits[:, None, :], axis=2), axis=1)
    shared_gate_pre = jnp.dot(second_normed, shared_gate, preferred_element_type=jnp.float32)
    shared_up_pre = jnp.dot(second_normed, shared_up, preferred_element_type=jnp.float32)
    shared_hidden = (jax.nn.silu(shared_gate_pre) * shared_up_pre).astype(jnp.bfloat16)
    shared_part = jnp.dot(shared_hidden, shared_down, preferred_element_type=jnp.float32)
    assigned = token_rows * TOPK
    flat_routes = routes.reshape(assigned)
    slot_hot = (flat_routes[:, None] == jnp.arange(slot_count, dtype=jnp.int32)[None, :]).astype(
        jnp.int32
    )
    slot_index = jnp.sum(slot_hot * jnp.cumsum(slot_hot, axis=0), axis=1) - 1
    position = flat_routes * capacity + slot_index
    owner = (
        jnp.full((slot_count * capacity,), assigned, jnp.int32)
        .at[position]
        .set(jnp.arange(assigned, dtype=jnp.int32))
    )
    padded_rows = jnp.concatenate([second_normed, jnp.zeros((1, width), jnp.bfloat16)], axis=0)
    outgoing = padded_rows[owner // TOPK].reshape(slot_count, capacity, width)
    arrived = to_experts(outgoing)
    expert_gate_pre = jnp.einsum(
        "emd,edf->emf", arrived, expert_gate, preferred_element_type=jnp.float32
    )
    expert_up_pre = jnp.einsum(
        "emd,edf->emf", arrived, expert_up, preferred_element_type=jnp.float32
    )
    expert_hidden = (jax.nn.silu(expert_gate_pre) * expert_up_pre).astype(jnp.bfloat16)
    expert_result = jnp.einsum(
        "emf,efd->emd", expert_hidden, expert_down, preferred_element_type=jnp.float32
    ).astype(jnp.bfloat16)
    returned = from_experts(expert_result).reshape(slot_count * capacity, width)
    picked = returned[position].reshape(token_rows, TOPK, width)
    routed_part = jnp.sum(gates[:, :, None] * picked.astype(jnp.float32), axis=1)
    mixture = of_everyone((shared_part + routed_part).astype(jnp.bfloat16), "tp").astype(
        jnp.float32
    )
    result = residual + mixture
    upstream = grad_out.astype(jnp.float32)
    shared_down_grad = jnp.einsum(
        "rf,rd->fd", shared_hidden, grad_out, preferred_element_type=jnp.float32
    )
    shared_hidden_grad = jnp.einsum(
        "rd,fd->rf", grad_out, shared_down, preferred_element_type=jnp.float32
    )
    shared_gate_step, shared_up_step = gated_grads(
        shared_gate_pre, shared_up_pre, shared_hidden_grad
    )
    shared_gate_grad = jnp.einsum(
        "rd,rf->df", second_normed, shared_gate_step, preferred_element_type=jnp.float32
    )
    shared_up_grad = jnp.einsum(
        "rd,rf->df", second_normed, shared_up_step, preferred_element_type=jnp.float32
    )
    shared_input = jnp.einsum(
        "rf,df->rd", shared_gate_step, shared_gate, preferred_element_type=jnp.float32
    ) + jnp.einsum("rf,df->rd", shared_up_step, shared_up, preferred_element_type=jnp.float32)
    gate_part = jnp.sum(upstream[:, None, :] * picked.astype(jnp.float32), axis=2)
    slot_grad = (
        (gates[:, :, None] * upstream[:, None, :]).astype(jnp.bfloat16).reshape(assigned, width)
    )
    padded_grad = jnp.concatenate([slot_grad, jnp.zeros((1, width), jnp.bfloat16)], axis=0)
    arrived_grad = to_experts(padded_grad[owner].reshape(slot_count, capacity, width))
    expert_down_grad = jnp.einsum(
        "emf,emd->efd", expert_hidden, arrived_grad, preferred_element_type=jnp.float32
    )
    expert_hidden_grad = jnp.einsum(
        "emd,efd->emf", arrived_grad, expert_down, preferred_element_type=jnp.float32
    )
    expert_gate_step, expert_up_step = gated_grads(
        expert_gate_pre, expert_up_pre, expert_hidden_grad
    )
    expert_gate_grad = jnp.einsum(
        "emd,emf->edf", arrived, expert_gate_step, preferred_element_type=jnp.float32
    )
    expert_up_grad = jnp.einsum(
        "emd,emf->edf", arrived, expert_up_step, preferred_element_type=jnp.float32
    )
    input_rows = (
        jnp.einsum(
            "emf,edf->emd", expert_gate_step, expert_gate, preferred_element_type=jnp.float32
        )
        + jnp.einsum("emf,edf->emd", expert_up_step, expert_up, preferred_element_type=jnp.float32)
    ).astype(jnp.bfloat16)
    back_rows = from_experts(input_rows).reshape(slot_count * capacity, width)
    routed_input = jnp.sum(
        back_rows[position].reshape(token_rows, TOPK, width).astype(jnp.float32), axis=1
    )
    second_grad, gate_grad = in_one((shared_input + routed_input, gate_part), "tp")
    weighted = jnp.sum(gates * gate_grad, axis=1, keepdims=True)
    selected_grad = gates * (gate_grad - weighted)
    logit_grad = jnp.sum(route_hot * selected_grad[:, :, None], axis=1).astype(jnp.bfloat16)
    router_grad = jnp.einsum(
        "rd,re->de", second_normed, logit_grad, preferred_element_type=jnp.float32
    )
    second_grad = second_grad + jnp.einsum(
        "re,de->rd", logit_grad, router_weight, preferred_element_type=jnp.float32
    )
    gain_two_grad, residual_back = norm_back(second_unit, second_inverse, norm2_gain, second_grad)
    residual_grad = upstream + residual_back
    attention_cot = residual_grad.astype(jnp.bfloat16)
    output_weight_grad = jnp.einsum(
        "rk,rd->kd", attended, attention_cot, preferred_element_type=jnp.float32
    )
    attended_cot = jnp.einsum(
        "rd,kd->rk", attention_cot, output_weight, preferred_element_type=jnp.float32
    ).astype(jnp.bfloat16)
    cot_heads = attended_cot.reshape(token_rows, local_heads, HEAD_DIM)
    query_grads = []
    key_grads = []
    value_grads = []
    for head in range(local_heads):
        scores = (
            jnp.einsum(
                "qd,kd->qk",
                query_heads[:, head],
                key_heads[:, head],
                preferred_element_type=jnp.float32,
            )
            * scale
        )
        exact = (
            jnp.exp(jnp.where(visible, scores, NEG_FILL) - highest_list[head]) / total_list[head]
        )
        weight_grad = jnp.einsum(
            "qd,kd->qk",
            cot_heads[:, head],
            value_heads[:, head],
            preferred_element_type=jnp.float32,
        )
        row_dot = jnp.sum(exact * weight_grad, axis=1, keepdims=True)
        score_grad = (exact * (weight_grad - row_dot) * scale).astype(jnp.bfloat16)
        query_grads.append(
            jnp.dot(score_grad, key_heads[:, head], preferred_element_type=jnp.float32)
        )
        key_grads.append(
            jnp.einsum(
                "qk,qd->kd", score_grad, query_heads[:, head], preferred_element_type=jnp.float32
            )
        )
        value_grads.append(
            jnp.einsum(
                "qk,qd->kd",
                exact.astype(jnp.bfloat16),
                cot_heads[:, head],
                preferred_element_type=jnp.float32,
            )
        )
    key_sum, value_sum = tuple(
        (
            part.astype(jnp.float32)
            for part in sent_together(
                (
                    jnp.concatenate(key_grads, axis=1).astype(jnp.bfloat16),
                    jnp.concatenate(value_grads, axis=1).astype(jnp.bfloat16),
                ),
                "ep",
                0,
                1,
            )
        )
    )
    query_pre_grad = (
        rotate(jnp.stack(query_grads, axis=1), cosine, -sine)
        .reshape(token_rows, local_heads * HEAD_DIM)
        .astype(jnp.bfloat16)
    )
    key_pre_grad = (
        rotate(key_sum.reshape(token_rows, local_heads, HEAD_DIM), cosine, -sine)
        .reshape(token_rows, local_heads * HEAD_DIM)
        .astype(jnp.bfloat16)
    )
    value_pre_grad = value_sum.astype(jnp.bfloat16)
    query_weight_grad = jnp.einsum(
        "rd,rk->dk", first_normed, query_pre_grad, preferred_element_type=jnp.float32
    )
    key_weight_grad = jnp.einsum(
        "rd,rk->dk", first_normed, key_pre_grad, preferred_element_type=jnp.float32
    )
    value_weight_grad = jnp.einsum(
        "rd,rk->dk", first_normed, value_pre_grad, preferred_element_type=jnp.float32
    )
    first_part = (
        jnp.einsum("rk,dk->rd", query_pre_grad, query_weight, preferred_element_type=jnp.float32)
        + jnp.einsum("rk,dk->rd", key_pre_grad, key_weight, preferred_element_type=jnp.float32)
        + jnp.einsum("rk,dk->rd", value_pre_grad, value_weight, preferred_element_type=jnp.float32)
    )
    first_grad = of_everyone(first_part.astype(jnp.bfloat16), "tp").astype(jnp.float32)
    gain_one_grad, input_back = norm_back(first_unit, first_inverse, norm1_gain, first_grad)
    input_grad = residual_grad + input_back
    (
        query_total,
        key_total,
        value_total,
        output_total,
        router_total,
        shared_gate_total,
        shared_up_total,
        shared_down_total,
        gain_one_total,
        gain_two_total,
    ) = sum_packed(
        (
            query_weight_grad,
            key_weight_grad,
            value_weight_grad,
            output_weight_grad,
            router_grad,
            shared_gate_grad,
            shared_up_grad,
            shared_down_grad,
            gain_one_grad,
            gain_two_grad,
        ),
        ("dp", "ep"),
        (0, 0, 0, 1, 0, 0, 0, 1, 0, 0),
    )
    expert_gate_total, expert_up_total, expert_down_total = (
        *tuple(
            (
                part.astype(jnp.float32)
                for part in sent_together(
                    (expert_gate_grad.astype(jnp.bfloat16), expert_up_grad.astype(jnp.bfloat16)),
                    "dp",
                    1,
                    0,
                )
            )
        ),
        lax.psum_scatter(
            expert_down_grad.astype(jnp.bfloat16), "dp", scatter_dimension=2, tiled=True
        ).astype(jnp.float32),
    )
    return (
        result.astype(jnp.bfloat16),
        input_grad,
        gain_one_total,
        gain_two_total,
        query_total,
        key_total,
        value_total,
        output_total,
        router_total,
        shared_gate_total,
        shared_up_total,
        shared_down_total,
        expert_gate_total,
        expert_up_total,
        expert_down_total,
    )


def solution(mesh):
    in_specs = (
        P(("dp", "ep"), None),
        P(("dp", "ep"), None),
        P("dp", None),
        P("dp", None),
        P("dp", None),
        P(("dp", "ep"), None),
        P(),
        P(),
        P(None, "tp"),
        P(None, "tp"),
        P(None, "tp"),
        P("tp", None),
        P(),
        P(None, "tp"),
        P(None, "tp"),
        P("tp", None),
        P("ep", None, "tp"),
        P("ep", None, "tp"),
        P("ep", "tp", None),
    )
    out_specs = (
        P(("dp", "ep"), None),
        P(("dp", "ep"), None),
        P(("dp", "ep")),
        P(("dp", "ep")),
        P(("dp", "ep"), "tp"),
        P(("dp", "ep"), "tp"),
        P(("dp", "ep"), "tp"),
        P("tp", ("dp", "ep")),
        P(("dp", "ep"), None),
        P(("dp", "ep"), "tp"),
        P(("dp", "ep"), "tp"),
        P("tp", ("dp", "ep")),
        P("ep", "dp", "tp"),
        P("ep", "dp", "tp"),
        P("ep", "tp", "dp"),
    )
    return jax.shard_map(local, mesh=mesh, in_specs=in_specs, out_specs=out_specs, check_vma=False)
```

profile of v0, /device:TPU:0, one launch (start us, length us, event | category | flops | bytes accessed | tf_op | source)
XLA Modules:
  0.0 1066.8 jit_solution(2340679738100101434)
XLA Ops:
  19.8 38.0 %all-gather.2.cloned.1.call-done = bf16[2048,1280]{1,0:T(8,128)(2,1)} async-done(((bf16[128,1280]{1,0:T(8,128)(2,1)}), bf16[2048,1280]{1,0:T(8,128)(2,1)}) %all-gather.2.cloned.1.call-update) | async-done | bytes 5242896 | tf_op jit(solution)/shard_map/all_gather | solution.py:21
  94.9 5.7 scatter_custom_fusion
  100.7 12.7 %all-to-all-done = f32[2,128,1280]{2,1,0:T(8,128)} async-done(((f32[2,128,1280]{2,1,0:T(8,128)}), f32[2,128,1280]{2,1,0:T(8,128)}, u32[]{:S(2)}, u32[]{:S(2)}) %all-to-all-start) | async-done | bytes 1310752 | tf_op jit(solution)/shard_map/all_to_all | solution.py:26
  117.1 5.5 gather_fusion
  140.1 8.6 gather_fusion.2
  148.7 13.0 %all-to-all-done.1 = bf16[64,16,1280]{2,1,0:T(8,128)(2,1)} async-done(((bf16[64,16,1280]{2,1,0:T(8,128)(2,1)}), bf16[64,16,1280]{2,1,0:T(8,128)(2,1)}, u32[]{:S(2)}, u32[]{:S(2)}) %all-to-all-start.1) | async-done | bytes 2621472 | tf_op jit(solution)/shard_map/all_to_all | solution.py:120
  161.7 7.7 all-to-all-start.4
  171.5 5.9 fusion.148
  180.1 23.8 %all-to-all-done.4 = bf16[64,16,1280]{2,1,0:T(8,128)(2,1)} async-done(((bf16[64,16,1280]{2,1,0:T(8,128)(2,1)}), bf16[64,16,1280]{2,1,0:T(8,128)(2,1)}, u32[]{:S(2)}, u32[]{:S(2)}) %all-to-all-start.4) | async-done | bytes 2621472 | tf_op jit(solution)/shard_map/all_to_all | solution.py:120
  206.0 7.5 multiply_convert_fusion.1
  218.6 8.3 all-to-all-start.2
  238.7 22.6 %all-to-all-done.2 = bf16[4,256,1280]{2,0,1:T(4,128)(2,1)} async-done(((bf16[4,256,1280]{2,0,1:T(4,128)(2,1)}), bf16[4,256,1280]{2,0,1:T(4,128)(2,1)}, u32[]{:S(2)}, u32[]{:S(2)}) %all-to-all-start.2) | async-done | bytes 2621472 | tf_op jit(solution)/shard_map/all_to_all | solution.py:124
  261.4 8.2 all-to-all-start.5
  278.7 8.4 gather_fusion.1
  312.8 8.4 gather_fusion.3
  349.2 15.4 %all-to-all-done.6 = f32[2,1,164736]{2,1,0:T(1,128)} async-done(((f32[2,1,164736]{2,1,0:T(1,128)}), f32[2,1,164736]{2,1,0:T(1,128)}, u32[]{:S(2)}, u32[]{:S(2)}) %all-to-all-start.6) | async-done | bytes 1317920 | tf_op jit(solution)/shard_map/all_to_all | solution.py:26
  364.5 8.1 reduce_sum.270
  403.2 7.8 copy.387
  412.3 5.7 convolution_convert_fusion
  427.8 16.2 %copy.373 = bf16[8,1280,448]{2,0,1:T(8,128)(2,1)} copy(bf16[8,1280,448]{1,2,0:T(8,128)(2,1)} %pad_maximum_fusion) | data formatting | bytes 18350080 | tf_op jit(solution)/shard_map/concatenate | solution.py:47
  472.4 6.2 copy.363
  478.5 6.4 reshape.453
  493.6 7.3 copy.358
  500.9 8.6 reshape.451
  545.8 5.9 copy.364
  551.8 6.0 copy.365
  557.7 6.0 copy.366
  564.8 98.5 %concatenate.55 = f32[64,79380]{0,1:T(8,128)} concatenate(f32[64,12800]{0,1:T(8,128)} %copy.364, f32[64,12800]{0,1:T(8,128)} %copy.365, f32[64,12800]{0,1:T(8,128)} %copy.366, f32[64,12800]{0,1:T(8,128)} %reshape.451, f32[64,1260]{0,1:T(8,128)S(1)} %copy-done.33, f32[64,8960]{0,1:T(8,128)} %copy.368, f32[64,8960]{0,1:T(8,128)} %copy.369, f32[64,8960]{0,1:T(8,128)} %reshape.453, ...), dimensions={1} | concatenate | bytes 40642560 | tf_op jit(solution)/shard_map/concatenate | solution.py:63
  663.3 30.2 %copy.394 = f32[64,79380]{1,0:T(8,128)} copy(f32[64,79380]{0,1:T(8,128)} %concatenate.55) | data formatting | bytes 40642560
  693.5 15.5 %pad.6.clone = f32[64,79872]{1,0:T(8,128)} pad(f32[64,79380]{1,0:T(8,128)} %copy.394, f32[]{:T(128)} %constant.22.clone.1), padding=0_0x0_492 | pad | bytes 40768516 | tf_op jit(solution)/shard_map/jit(_pad)/pad | solution.py:65
  709.0 16.4 %reshape.456 = f32[39936,128]{1,0:T(8,128)} reshape(f32[64,79872]{1,0:T(8,128)} %pad.6.clone) | data formatting | bytes 40894464 | tf_op jit(solution)/shard_map/reshape | solution.py:65
  737.8 312.3 %reduce-scatter.7.cloned.1.call-done = f32[624,128]{1,0:T(8,128)} async-done(((f32[39936,128]{1,0:T(8,128)}), f32[624,128]{1,0:T(8,128)}) %reduce-scatter.7.cloned.1.call-update) | async-done | bytes 319504 | tf_op jit(solution)/shard_map/reduce_scatter | solution.py:66
  (389 shorter events, 294.6 us)
Async XLA Ops:
  7.2 81.3 %copy-start = (bf16[640,1280]{1,0:T(8,128)(2,1)S(1)}, bf16[640,1280]{1,0:T(8,128)(2,1)}, u32[]{:S(2)}) copy-start(bf16[640,1280]{1,0:T(8,128)(2,1)} %param.30) | copy-start | bytes 4915204
  7.2 50.6 %all-gather.2.cloned.1.call-start = ((), (), s32[]{:S(2)}) async-start(), calls=%async_computation.12 | async-start | bytes 5570560 | tf_op jit(solution)/shard_map/all_gather | solution.py:21
  18.7 44.4 %copy-start.42 = (s32[64,7,128]{2,0,1:T(8,128)}, s32[64,7,128]{2,0,1:T(8,128)S(1)}, u32[]{:S(2)}) copy-start(s32[64,7,128]{2,0,1:T(8,128)S(1)} %reduce-window.6) | copy-start | bytes 688132
  69.2 16.9 %copy-start.9 = (f32[128,2048]{1,0:T(8,128)}, f32[128,2048]{1,0:T(8,128)S(1)}, u32[]{:S(2)}) copy-start(f32[128,2048]{1,0:T(8,128)S(1)} %get-tuple-element.173) | copy-start | bytes 3145732
  74.6 8.6 copy-start.65
  75.9 10.6 copy-start.69
  90.0 26.9 %copy-start.61 = (f32[1280]{0:T(1024)S(1)}, f32[1280]{0:T(1024)}, u32[]{:S(2)}) copy-start(f32[1280]{0:T(1024)} %param.26) | copy-start | bytes 15364
  90.0 23.3 %all-to-all-start = ((f32[2,128,1280]{2,1,0:T(8,128)}), f32[2,128,1280]{2,1,0:T(8,128)}, u32[]{:S(2)}, u32[]{:S(2)}) async-start(f32[2,128,1280]{2,1,0:T(8,128)} %broadcast_in_dim.28), calls=%async_computation | async-start | bytes 2621440 | tf_op jit(solution)/shard_map/all_to_all | solution.py:26
  116.9 261.6 %copy-start.8 = (f32[128,1280]{1,0:T(8,128)}, f32[128,1280]{1,0:T(8,128)S(1)}, u32[]{:S(2)}) copy-start(f32[128,1280]{1,0:T(8,128)S(1)} %get-tuple-element.127) | copy-start | bytes 1966084
  122.6 39.1 %all-to-all-start.1 = ((bf16[64,16,1280]{2,1,0:T(8,128)(2,1)}), bf16[64,16,1280]{2,1,0:T(8,128)(2,1)}, u32[]{:S(2)}, u32[]{:S(2)}) async-start(bf16[64,16,1280]{2,1,0:T(8,128)(2,1)} %bitcast.304), calls=%async_computation.1 | async-start | bytes 5242880 | tf_op jit(solution)/shard_map/all_to_all | solution.py:120
  161.7 42.2 %all-to-all-start.4 = ((bf16[64,16,1280]{2,1,0:T(8,128)(2,1)}), bf16[64,16,1280]{2,1,0:T(8,128)(2,1)}, u32[]{:S(2)}, u32[]{:S(2)}) async-start(bf16[64,16,1280]{2,1,0:T(8,128)(2,1)} %bitcast.305), calls=%async_computation.4 | async-start | bytes 5242880 | tf_op jit(solution)/shard_map/all_to_all | solution.py:120
  169.4 8.0 slice-start.2
  171.5 5.9 copy-start.2
  203.8 9.6 slice-start
  205.9 7.5 copy-start.7
  205.9 7.5 slice-start.1
  218.6 42.7 %all-to-all-start.2 = ((bf16[4,256,1280]{2,0,1:T(4,128)(2,1)}), bf16[4,256,1280]{2,0,1:T(4,128)(2,1)}, u32[]{:S(2)}, u32[]{:S(2)}) async-start(bf16[4,256,1280]{2,0,1:T(4,128)(2,1)} %copy.342), calls=%async_computation.2 | async-start | bytes 5242880 | tf_op jit(solution)/shard_map/all_to_all | solution.py:124
  261.4 42.6 %all-to-all-start.5 = ((bf16[4,256,1280]{2,0,1:T(4,128)(2,1)}), bf16[4,256,1280]{2,0,1:T(4,128)(2,1)}, u32[]{:S(2)}, u32[]{:S(2)}) async-start(bf16[4,256,1280]{2,0,1:T(4,128)(2,1)} %copy.346), calls=%async_computation.5 | async-start | bytes 5242880 | tf_op jit(solution)/shard_map/all_to_all | solution.py:124
  304.8 32.8 %all-to-all-start.3 = ((bf16[2,128,1280]{2,1,0:T(8,128)(2,1)}), bf16[2,128,1280]{2,1,0:T(8,128)(2,1)}, u32[]{:S(2)}, u32[]{:S(2)}) async-start(bf16[2,128,1280]{2,1,0:T(8,128)(2,1)} %broadcast_in_dim.31), calls=%async_computation.3 | async-start | bytes 1310720 | tf_op jit(solution)/shard_map/all_to_all | solution.py:26
  341.8 22.7 %all-to-all-start.6 = ((f32[2,1,164736]{2,1,0:T(1,128)}), f32[2,1,164736]{2,1,0:T(1,128)}, u32[]{:S(2)}, u32[]{:S(2)}) async-start(f32[2,1,164736]{2,1,0:T(1,128)} %broadcast_in_dim.33), calls=%async_computation.6 | async-start | bytes 2635776 | tf_op jit(solution)/shard_map/all_to_all | solution.py:26
  346.6 170.0 %reduce-scatter.13.cloned.1.call-start = ((), (), s32[]{:S(2)}) async-start(), calls=%async_computation.16 | async-start | bytes 5570560
  349.2 29.3 %copy-start.49 = (bf16[1280,63]{0,1:T(8,128)(2,1)S(1)}, bf16[1280,63]{0,1:T(8,128)(2,1)}, u32[]{:S(2)}) copy-start(bf16[1280,63]{0,1:T(8,128)(2,1)} %param.31) | copy-start | bytes 483844
  349.2 29.4 %copy-start.68 = (f32[128]{0:T(128)S(1)}, f32[128]{0:T(128)}, u32[]{:S(2)}) copy-start(f32[128]{0:T(128)} %copy-done.67) | copy-start | bytes 1540
  411.1 314.3 %reduce-scatter.11.cloned.1.call-start = ((), (), s32[]{:S(2)}) async-start(), calls=%async_computation.15 | async-start | bytes 6553600 | tf_op jit(solution)/shard_map/reduce_scatter | solution.py:446
  418.0 311.8 %reduce-scatter.9.cloned.1.call-start = ((), (), s32[]{:S(2)}) async-start(), calls=%async_computation.14 | async-start | bytes 13107200 | tf_op jit(solution)/shard_map/reduce_scatter | solution.py:48
  500.9 10.1 copy-start.39
  500.9 11.5 %copy-start.37 = (bf16[128,2048]{1,0:T(8,128)(2,1)S(1)}, bf16[128,2048]{1,0:T(8,128)(2,1)}, u32[]{:S(2)}) copy-start(bf16[128,2048]{1,0:T(8,128)(2,1)} %copy-done.36) | copy-start | bytes 1572868
  511.0 6.8 copy-start.57
  511.0 6.8 copy-start.60
  521.4 42.3 %all-to-all-start.7 = ((bf16[2,128,1280]{2,1,0:T(8,128)(2,1)}), bf16[2,128,1280]{2,1,0:T(8,128)(2,1)S(1)}, u32[]{:S(2)}, u32[]{:S(2)}) async-start(bf16[2,128,1280]{2,1,0:T(8,128)(2,1)} %broadcast_in_dim.34), calls=%async_computation.7 | async-start | bytes 1310720 | tf_op jit(solution)/shard_map/all_to_all | solution.py:26
  524.9 525.1 %reduce-scatter.7.cloned.1.call-start = ((), (), s32[]{:S(2)}) async-start(), calls=%async_computation.13 | async-start | bytes 20766720 | tf_op jit(solution)/shard_map/reduce_scatter | solution.py:66
  735.5 324.6 %copy-start.1 = (bf16[640,1280]{1,0:T(8,128)(2,1)S(1)}, bf16[640,1280]{1,0:T(8,128)(2,1)}, u32[]{:S(2)}) copy-start(bf16[640,1280]{1,0:T(8,128)(2,1)} %param.30) | copy-start | bytes 4915204
  (70 other events, 226.2 us)
Sparse Core Ops, SparseCore 0:
  15.9 41.9 all-gather.1
  411.2 71.9 reduce-scatter.12
  485.6 53.8 reduce-scatter.10
  541.8 97.1 reduce-scatter.8
  725.5 324.4 reduce-scatter.6
where the time goes:
time: 1080 us; the launch traced here: 1070 us
  waiting for transfers between devices  443 us (41%)
  local copies, waits for them, and re-layouts  402 us (37%)
  matrix products  106 us (10%)
  other arithmetic  53.9 us (5%)
  starting transfers between devices  46.8 us (4%)
  between operations  15.5 us (1%)
    reduce_scatter x1, waiting for transfers between devices, sum_packed(): lax.psum_scatter(lines, axis, tiled=True).reshape(-1)  312 us
    concatenate x1, local copies, waits for them, and re-layouts, sum_packed(): lines = jnp.concatenate([b.reshape(size, -1) for b in blocks], axis=1)  98.5 us
    unnamed x184, local copies, waits for them, and re-layouts  53.3 us
    another operation x12, local copies, waits for them, and re-layouts, sum_packed(): lines = jnp.concatenate([b.reshape(size, -1) for b in blocks], axis=1)  50.1 us
    all_gather x1, waiting for transfers between devices, side_by_side(): lax.all_gather(both, axis, axis=dim, tiled=True)  38 us
    all_to_all x2, waiting for transfers between devices, to_experts(): return lax.all_to_all(buffer, 'ep', split_axis=0, concat_axis=1, tiled=True)  36.8 us
    all_to_all x4, waiting for transfers between devices, from_everyone(): return lax.all_to_all(copies, axis, split_axis=0, concat_axis=0, tiled=True)  28.1 us
    all_to_all x2, waiting for transfers between devices, from_experts(): return lax.all_to_all(buffer, 'ep', split_axis=1, concat_axis=0, tiled=True)  27.9 us
  transfers between devices with their start and end apart: 13, of which 8 were waited for; matrix products, arithmetic and copies ran while one was open for 40% of the time, Pallas kernels for 0%

commit v1 on v0

v1 whole, which is shorter than its diff:
```python
import jax
import jax.numpy as jnp
from jax import lax
from jax.experimental import pallas as pl
from jax.experimental.pallas import tpu as pltpu
from jax.sharding import Mesh, PartitionSpec as P

F32 = jnp.float32
BF16 = jnp.bfloat16
HEAD_DIM = 128
TOPK = 7
EPSILON = 1e-06
NEG_FILL = -1e30
BASE = 10000.0
SCALE = HEAD_DIM ** (-0.5)

T = 128
D = 1280
HEADS = 5
HW = HEADS * HEAD_DIM
FF = 448
E = 4
CAP = 16
BLOCKS = 16
KEYS = 1280
EXTRA = 128

EP = ("yl", "z", "c")
VMEM = pl.BlockSpec(memory_space=pltpu.VMEM)
SMEM = pl.BlockSpec(memory_space=pltpu.SMEM)
ANY = pl.BlockSpec(memory_space=pl.ANY)


def params(mib, **more):
    return pltpu.CompilerParams(vmem_limit_bytes=mib << 20, **more)


def cost(flops, moved):
    return pl.CostEstimate(flops=int(flops), bytes_accessed=int(moved), transcendentals=0)


def dot(a, b):
    return lax.dot_general(a, b, (((1,), (0,)), ((), ())), preferred_element_type=F32)


def dot_nt(a, b):
    return lax.dot_general(a, b, (((1,), (1,)), ((), ())), preferred_element_type=F32)


def dot_tn(a, b):
    return lax.dot_general(a, b, (((0,), (0,)), ((), ())), preferred_element_type=F32)


def split3(v):
    first = v.astype(BF16)
    rest = v - first.astype(F32)
    second = rest.astype(BF16)
    return first, second, (rest - second.astype(F32)).astype(BF16)


def lanes(shape):
    return lax.broadcasted_iota(jnp.int32, shape, 1)


def rows(shape):
    return lax.broadcasted_iota(jnp.int32, shape, 0)


def turn(values, cosine, sine):
    parts = []
    for h in range(HEADS):
        z = values[:, h * 128 : (h + 1) * 128]
        parts.append(z * cosine + pltpu.roll(z, 64, 1) * sine)
    return jnp.concatenate(parts, axis=1)


def per_token(columns):
    lane = lanes((T, EXTRA))
    out = jnp.zeros((T, EXTRA), F32)
    for j, column in enumerate(columns):
        out = jnp.where(lane == j, column.astype(F32), out)
    return out.astype(BF16)


def project_kernel(x_ref, g_ref, wq_ref, wk_ref, wv_ref, cos_ref, sin_ref, routes_ref, dy_ref, h1_ref, q_ref, kv_ref, dyp_ref, hot_ref):
    x = x_ref[...].astype(F32)
    inverse = lax.rsqrt(jnp.mean(x * x, axis=1, keepdims=True) + EPSILON)
    h1 = (x * inverse * g_ref[...]).astype(BF16)
    h1_ref[...] = h1
    cosine, sine = cos_ref[...], sin_ref[...]
    kv_ref[:, :HW] = turn(dot(h1, wk_ref[...]), cosine, sine).astype(BF16)
    kv_ref[:, HW:] = dot(h1, wv_ref[...]).astype(BF16)
    q_ref[...] = turn(dot(h1, wq_ref[...]), cosine, sine).astype(BF16)
    lane = lanes((T, EXTRA))
    routes = routes_ref[...]
    hot = jnp.zeros((T, EXTRA), F32)
    for j in range(TOPK):
        hot = jnp.where(lane == routes[:, j : j + 1], 1.0, hot)
    hot_ref[...] = hot
    before = (lanes((T, T)) < rows((T, T))).astype(BF16)
    slot = dot(before, hot.astype(BF16))
    dyp_ref[:, :D] = dy_ref[...]
    dyp_ref[:, D:] = jnp.where(hot > 0.5, slot, -1.0).astype(BF16)


def project(x, gain, wq, wk, wv, cosine, sine, routes, dy):
    return pl.pallas_call(
        project_kernel,
        out_shape=(
            jax.ShapeDtypeStruct((T, D), BF16),
            jax.ShapeDtypeStruct((T, HW), BF16),
            jax.ShapeDtypeStruct((T, 2 * HW), BF16),
            jax.ShapeDtypeStruct((T, D + EXTRA), BF16),
            jax.ShapeDtypeStruct((T, EXTRA), F32),
        ),
        in_specs=[VMEM] * 9,
        out_specs=(VMEM,) * 5,
        compiler_params=params(24),
        cost_estimate=cost(2 * T * D * 3 * HW, 6e6),
        name="project",
    )(x, gain, wq, wk, wv, cosine, sine, routes, dy)


def attend_kernel(at_ref, q_ref, kv_hbm, bias_ref, wo_ref, o_ref, part_ref, qp_ref, kvs, sem):
    start = pl.multiple_of(at_ref[0], 128)
    copy = pltpu.make_async_copy(kv_hbm.at[pl.ds(start, KEYS), :], kvs, sem)
    copy.start()
    copy.wait()
    stats, outs = [], []
    for h in range(HEADS):
        q = q_ref[:, h * 128 : (h + 1) * 128]
        s = dot_nt(q, kvs[:, h * 128 : (h + 1) * 128]) * SCALE + bias_ref[...]
        high = jnp.max(s, axis=1, keepdims=True)
        e = jnp.exp(s - high)
        total = jnp.sum(e, axis=1, keepdims=True)
        p = (e * (1.0 / total)).astype(BF16)
        outs.append(dot(p, kvs[:, HW + h * 128 : HW + (h + 1) * 128]))
        stats += list(split3((high + jnp.log(total)) * (-1.0 / SCALE)))
    o = jnp.concatenate(outs, axis=1)
    o_ref[...] = o
    part_ref[...] = dot(o.astype(BF16), wo_ref[...]).astype(BF16)
    qp_ref[:, :HW] = q_ref[...]
    qp_ref[:, HW:] = per_token(stats)


def attend(at, q, kv_all, bias, wo):
    return pl.pallas_call(
        attend_kernel,
        out_shape=(
            jax.ShapeDtypeStruct((T, HW), F32),
            jax.ShapeDtypeStruct((T, D), BF16),
            jax.ShapeDtypeStruct((T, HW + EXTRA), BF16),
        ),
        in_specs=[SMEM, VMEM, ANY, VMEM, VMEM],
        out_specs=(VMEM,) * 3,
        scratch_shapes=[pltpu.VMEM((KEYS, 2 * HW), BF16), pltpu.SemaphoreType.DMA],
        compiler_params=params(32),
        cost_estimate=cost(4 * T * KEYS * HW + 2 * T * HW * D, 6e6),
        name="attend",
    )(at, q, kv_all, bias, wo)


def gate_kernel(x_ref, a_ref, b_ref, g_ref, wr_ref, hot_ref, r_ref, h2p_ref, gates_ref):
    r = x_ref[...].astype(F32) + (a_ref[...].astype(F32) + b_ref[...].astype(F32))
    r_ref[...] = r
    inverse = lax.rsqrt(jnp.mean(r * r, axis=1, keepdims=True) + EPSILON)
    h2 = (r * inverse * g_ref[...]).astype(BF16)
    hot = hot_ref[...] > 0.5
    logits = jnp.where(hot, dot(h2, wr_ref[...]), NEG_FILL)
    e = jnp.where(hot, jnp.exp(logits - jnp.max(logits, axis=1, keepdims=True)), 0.0)
    gates = e / jnp.sum(e, axis=1, keepdims=True)
    gates_ref[...] = gates
    first = gates.astype(BF16).astype(F32)
    h2p_ref[:, :D] = h2
    h2p_ref[:, D:] = (first + pltpu.roll(gates - first, 64, 1)).astype(BF16)


def gate(x, a, b, gain, wr, hot):
    return pl.pallas_call(
        gate_kernel,
        out_shape=(
            jax.ShapeDtypeStruct((T, D), F32),
            jax.ShapeDtypeStruct((T, D + EXTRA), BF16),
            jax.ShapeDtypeStruct((T, EXTRA), F32),
        ),
        in_specs=[VMEM] * 6,
        out_specs=(VMEM,) * 3,
        compiler_params=params(16),
        cost_estimate=cost(2 * T * D * 128, 2e6),
        name="gate",
    )(x, a, b, gain, wr, hot)


def silu_parts(gate_pre):
    sigmoid = 1.0 / (1.0 + jnp.exp(-gate_pre))
    return gate_pre * sigmoid, sigmoid * (1.0 + gate_pre * (1.0 - sigmoid))


def shared_kernel(h2p_ref, dy_ref, wg_ref, wu_ref, wd_ref, out_ref, dh_ref, sh_ref, dsg_ref, dsu_ref):
    h2 = h2p_ref[:, :D]
    sg = dot(h2, wg_ref[...])
    su = dot(h2, wu_ref[...])
    act, slope = silu_parts(sg)
    sh = (act * su).astype(BF16)
    sh_ref[...] = sh
    out_ref[...] = dot(sh, wd_ref[...])
    dsh = dot_nt(dy_ref[...], wd_ref[...])
    dsg = (dsh * su * slope).astype(BF16)
    dsu = (dsh * act).astype(BF16)
    dsg_ref[...] = dsg
    dsu_ref[...] = dsu
    dh_ref[...] = dot_nt(dsg, wg_ref[...]) + dot_nt(dsu, wu_ref[...])


def shared(h2p, dy, wg, wu, wd):
    hidden = jax.ShapeDtypeStruct((T, FF), BF16)
    return pl.pallas_call(
        shared_kernel,
        out_shape=(jax.ShapeDtypeStruct((T, D), F32), jax.ShapeDtypeStruct((T, D), F32), hidden, hidden, hidden),
        in_specs=[VMEM] * 5,
        out_specs=(VMEM,) * 5,
        compiler_params=params(24),
        cost_estimate=cost(12 * T * D * FF, 5e6),
        name="shared",
    )(h2p, dy, wg, wu, wd)


def block_of(rank, entry, other):
    yl, z, c = rank // 8, (rank // 2) % 4, rank % 2
    dz = (0, 3, 1, 2)[entry % 4]
    return (((yl + entry // 4) % 2) * 4 + (z + dz) % 4) * 2 + (c + other) % 2


def experts_kernel(
    rank_ref, h2_ref, dy_ref, wg_ref, wu_ref, wd_ref,
    xb_ref, dyo_ref, eh_ref, dgu_ref, own_ref, oth_ref, yown_ref, yoth_ref,
    pt, xs, dys, gs, ys, dbs,
):
    e = pl.program_id(0)
    rank = rank_ref[0]

    @pl.when(e == 0)
    def _():
        spread = (rows((EXTRA, E * CAP)) == rank * E + lanes((EXTRA, E * CAP)) // CAP).astype(BF16)
        place = (lanes((T, E * CAP)) % CAP).astype(F32)
        named = rank * E + rows((E * CAP, EXTRA)) // CAP
        column = lanes((E * CAP, EXTRA))
        mine = (column == named) | (column == named + 64)

        def one(k, carry):
            at = pl.ds(pl.multiple_of(k * T, T), T)
            slot = dot(dy_ref[at, D:], spread)
            hot = (slot == place).astype(BF16)
            pt[k] = hot
            x = dot_tn(hot, h2_ref[at, :])
            dy = dot_tn(hot, dy_ref[at, :D]).astype(BF16)
            g = jnp.sum(jnp.where(mine, x[:, D:], 0.0), axis=1, keepdims=True)
            g = jnp.broadcast_to(g, (E * CAP, 128))
            x = x[:, :D].astype(BF16)
            for i in range(E):
                to = pl.ds(pl.multiple_of(k * CAP, CAP), CAP)
                xs[i, to, :] = x[i * CAP : (i + 1) * CAP]
                dys[i, to, :] = dy[i * CAP : (i + 1) * CAP]
                gs[i, to, :] = g[i * CAP : (i + 1) * CAP]
            return carry

        lax.fori_loop(0, BLOCKS, one, 0)

    x = xs[e]
    eg = dot(x, wg_ref[0])
    eu = dot(x, wu_ref[0])
    act, slope = silu_parts(eg)
    eh = (act * eu).astype(BF16)
    y = dot(eh, wd_ref[0]).astype(BF16).astype(F32)
    g = gs[e][:, :1]
    dy = dys[e].astype(F32)
    dgate = jnp.sum(dy * y, axis=1, keepdims=True)
    ys[e] = (g * y).astype(BF16)
    dyg = (g * dy).astype(BF16)
    deh = dot_nt(dyg, wd_ref[0])
    deg = (deh * eu * slope).astype(BF16)
    deu = (deh * act).astype(BF16)
    db = dot_nt(deg, wg_ref[0]) + dot_nt(deu, wu_ref[0])
    dbs[e, :, :D] = db.astype(BF16)
    column = lanes((BLOCKS * CAP, EXTRA))
    first = dgate.astype(BF16).astype(F32)
    own_column = rank * E + e
    placed = jnp.where(column == own_column, first, jnp.where(column == own_column + 64, dgate - first, 0.0))
    dbs[e, :, D:] = placed.astype(BF16)
    xb_ref[0] = x
    dyo_ref[0] = dyg
    dgu_ref[0] = jnp.concatenate([deg, deu], axis=1)
    none = jnp.zeros((BLOCKS * CAP, FF), BF16)

    @pl.when(e % 2 == 0)
    def _():
        eh_ref[0] = jnp.concatenate([eh, none], axis=1)

    @pl.when(e % 2 == 1)
    def _():
        eh_ref[0] = jnp.concatenate([none, eh], axis=1)

    @pl.when(e == E - 1)
    def _():
        for other, to, yto in ((0, own_ref, yown_ref), (1, oth_ref, yoth_ref)):
            for j in range(8):
                k = block_of(rank, j, other)
                hot = pt[k]
                at = pl.ds(pl.multiple_of(k * CAP, CAP), CAP)
                to[j] = dot(hot, jnp.concatenate([dbs[i, at, :] for i in range(E)], axis=0)).astype(BF16)
                yto[j] = dot(hot, jnp.concatenate([ys[i, at, :] for i in range(E)], axis=0)).astype(BF16)


def experts(rank, h2_all, dy_all, wg, wu, wd):
    n = BLOCKS * CAP
    per = lambda shape: pl.BlockSpec((1, *shape), lambda e: (e, 0, 0))
    whole = lambda shape: pl.BlockSpec(shape, lambda e: (0,) * len(shape), pipeline_mode=pl.Buffered(1))
    return pl.pallas_call(
        experts_kernel,
        out_shape=(
            jax.ShapeDtypeStruct((E, n, D), BF16),
            jax.ShapeDtypeStruct((E, n, D), BF16),
            jax.ShapeDtypeStruct((E, n, 2 * FF), BF16),
            jax.ShapeDtypeStruct((E, n, 2 * FF), BF16),
            jax.ShapeDtypeStruct((8, T, D + EXTRA), BF16),
            jax.ShapeDtypeStruct((8, T, D + EXTRA), BF16),
            jax.ShapeDtypeStruct((8, T, D), BF16),
            jax.ShapeDtypeStruct((8, T, D), BF16),
        ),
        grid=(E,),
        in_specs=[
            SMEM,
            whole((BLOCKS * T, D + EXTRA)),
            whole((BLOCKS * T, D + EXTRA)),
            per((D, FF)),
            per((D, FF)),
            per((FF, D)),
        ],
        out_specs=(
            per((n, D)), per((n, D)), per((n, 2 * FF)), per((n, 2 * FF)),
            whole((8, T, D + EXTRA)), whole((8, T, D + EXTRA)), whole((8, T, D)), whole((8, T, D)),
        ),
        scratch_shapes=[
            pltpu.VMEM((BLOCKS, T, E * CAP), BF16),
            pltpu.VMEM((E, n, D), BF16),
            pltpu.VMEM((E, n, D), BF16),
            pltpu.VMEM((E, n, 128), F32),
            pltpu.VMEM((E, n, D), BF16),
            pltpu.VMEM((E, n, D + EXTRA), BF16),
        ],
        compiler_params=params(58, dimension_semantics=("arbitrary",)),
        cost_estimate=cost(2 * E * n * D * FF * 7, 5e7),
        name="experts",
    )(rank, h2_all, dy_all, wg, wu, wd)


def expert_grads_kernel(x_ref, dy_ref, eh_ref, dgu_ref, gu_ref, down_ref):
    gu_ref[:, : 2 * FF] = dot_tn(x_ref[0], dgu_ref[0]).astype(BF16)
    gu_ref[:, 2 * FF :] = dot_tn(x_ref[1], dgu_ref[1]).astype(BF16)
    down_ref[...] = (dot_tn(dy_ref[0], eh_ref[0]) + dot_tn(dy_ref[1], eh_ref[1])).astype(BF16)


def expert_grads(x, dy, eh, dgu):
    n = BLOCKS * CAP
    per = lambda width: pl.BlockSpec((2, n, width), lambda p: (p, 0, 0))
    return pl.pallas_call(
        expert_grads_kernel,
        out_shape=(
            jax.ShapeDtypeStruct((D, E * 2 * FF), BF16),
            jax.ShapeDtypeStruct((D, E * FF), BF16),
        ),
        grid=(E // 2,),
        in_specs=[per(D), per(D), per(2 * FF), per(2 * FF)],
        out_specs=(
            pl.BlockSpec((D, 4 * FF), lambda p: (0, p)),
            pl.BlockSpec((D, 2 * FF), lambda p: (0, p)),
        ),
        compiler_params=params(56, dimension_semantics=("arbitrary",)),
        cost_estimate=cost(2 * E * n * D * FF * 3, 3e7),
        name="expert_grads",
    )(x, dy, eh, dgu)


def middle_kernel(a_ref, b_ref, r_ref, dy_ref, h2p_ref, gates_ref, g_ref, wr_ref, wo_ref, o_ref, dr_ref, da_ref, dop_ref, dlog_ref, gain_ref):
    both = a_ref[...].astype(F32) + b_ref[...].astype(F32)
    gates = gates_ref[...]
    dgate = both[:, D:] + pltpu.roll(both[:, D:], 64, 1)
    dsel = gates * (dgate - jnp.sum(gates * dgate, axis=1, keepdims=True))
    dlog = dsel.astype(BF16)
    dlog_ref[...] = dlog
    dh2 = both[:, :D] + dot_nt(dlog, wr_ref[...])
    r = r_ref[...]
    inverse = lax.rsqrt(jnp.mean(r * r, axis=1, keepdims=True) + EPSILON)
    unit = r * inverse
    gain_ref[...] = (dh2 * unit).astype(BF16)
    e2 = dh2 * g_ref[...]
    dr = dy_ref[...].astype(F32) + inverse * (e2 - unit * jnp.mean(e2 * unit, axis=1, keepdims=True))
    dr_ref[...] = dr
    da = dr.astype(BF16)
    da_ref[...] = da
    do = dot_nt(da, wo_ref[...]).astype(BF16)
    dop_ref[:, :HW] = do
    stats = []
    both = do.astype(F32) * o_ref[...]
    for h in range(HEADS):
        stats += list(split3(-jnp.sum(both[:, h * 128 : (h + 1) * 128], axis=1, keepdims=True)))
    dop_ref[:, HW:] = per_token(stats)


def middle(a, b, r, dy, h2p, gates, gain, wr, wo, o):
    return pl.pallas_call(
        middle_kernel,
        out_shape=(
            jax.ShapeDtypeStruct((T, D), F32),
            jax.ShapeDtypeStruct((T, D), BF16),
            jax.ShapeDtypeStruct((T, HW + EXTRA), BF16),
            jax.ShapeDtypeStruct((T, EXTRA), BF16),
            jax.ShapeDtypeStruct((T, D), BF16),
        ),
        in_specs=[VMEM] * 10,
        out_specs=(VMEM,) * 5,
        compiler_params=params(24),
        cost_estimate=cost(2 * T * D * (HW + 128), 5e6),
        name="middle",
    )(a, b, r, dy, h2p, gates, gain, wr, wo, o)


def attend_back_kernel(
    at_ref, qp_ref, kv_ref, dop_ref, kv_hbm, q_hbm, do_hbm, qbias_ref, kbias_ref, cos_ref, sin_ref, wq_ref, wk_ref, wv_ref,
    dqkv_ref, part_ref, kvs, qs, dos, sems,
):
    keys_at = pl.multiple_of(at_ref[0], 128)
    queries_at = pl.multiple_of(at_ref[1], 128)
    copies = [
        pltpu.make_async_copy(kv_hbm.at[pl.ds(keys_at, KEYS), :], kvs, sems.at[0]),
        pltpu.make_async_copy(q_hbm.at[pl.ds(queries_at, KEYS), :], qs, sems.at[1]),
        pltpu.make_async_copy(do_hbm.at[pl.ds(queries_at, KEYS), :], dos, sems.at[2]),
    ]
    for copy in copies:
        copy.start()
    for copy in copies:
        copy.wait()
    lane = lanes((T, EXTRA))
    q_extra = qp_ref[:, HW:].astype(F32)
    do_extra = dop_ref[:, HW:].astype(F32)
    dqs, dks, dvs = [], [], []
    for h in range(HEADS):
        cut = slice(h * 128, (h + 1) * 128)
        vcut = slice(HW + h * 128, HW + (h + 1) * 128)
        mine = (lane >= 3 * h) & (lane < 3 * h + 3)
        less = jnp.sum(jnp.where(mine, q_extra, 0.0), axis=1, keepdims=True)
        less_dot = jnp.sum(jnp.where(mine, do_extra, 0.0), axis=1, keepdims=True)
        p = jnp.exp((dot_nt(qp_ref[:, cut], kvs[:, cut]) + less) * SCALE + qbias_ref[...])
        dp = dot_nt(dop_ref[:, cut], kvs[:, vcut]) + less_dot
        ds = (p * dp * SCALE).astype(BF16)
        dqs.append(dot(ds, kvs[:, cut]))
        ones = mine.astype(BF16)
        k_wide = jnp.concatenate([kv_ref[:, cut], ones], axis=1)
        v_wide = jnp.concatenate([kv_ref[:, vcut], ones], axis=1)
        q_wide = jnp.concatenate([qs[:, cut], qs[:, HW:]], axis=1)
        do_wide = jnp.concatenate([dos[:, cut], dos[:, HW:]], axis=1)
        pt = jnp.exp(dot_nt(k_wide, q_wide) * SCALE + kbias_ref[...])
        dst = (pt * dot_nt(v_wide, do_wide) * SCALE).astype(BF16)
        dks.append(dot(dst, qs[:, cut]))
        dvs.append(dot(pt.astype(BF16), dos[:, cut]))
    cosine, sine = cos_ref[...], -sin_ref[...]
    dq = turn(jnp.concatenate(dqs, axis=1), cosine, sine).astype(BF16)
    dk = turn(jnp.concatenate(dks, axis=1), cosine, sine).astype(BF16)
    dv = jnp.concatenate(dvs, axis=1).astype(BF16)
    dqkv_ref[:, :HW] = dq
    dqkv_ref[:, HW : 2 * HW] = dk
    dqkv_ref[:, 2 * HW :] = dv
    part_ref[...] = (dot_nt(dq, wq_ref[...]) + dot_nt(dk, wk_ref[...]) + dot_nt(dv, wv_ref[...])).astype(BF16)


def attend_back(at, qp, kv, dop, kv_all, q_all, do_all, qbias, kbias, cosine, sine, wq, wk, wv):
    return pl.pallas_call(
        attend_back_kernel,
        out_shape=(jax.ShapeDtypeStruct((T, 3 * HW), BF16), jax.ShapeDtypeStruct((T, D), BF16)),
        in_specs=[SMEM, VMEM, VMEM, VMEM, ANY, ANY, ANY] + [VMEM] * 7,
        out_specs=(VMEM,) * 2,
        scratch_shapes=[
            pltpu.VMEM((KEYS, 2 * HW), BF16),
            pltpu.VMEM((KEYS, HW + EXTRA), BF16),
            pltpu.VMEM((KEYS, HW + EXTRA), BF16),
            pltpu.SemaphoreType.DMA((3,)),
        ],
        compiler_params=params(48),
        cost_estimate=cost(16 * T * KEYS * HW + 6 * T * HW * D, 2e7),
        name="attend_back",
    )(at, qp, kv, dop, kv_all, q_all, do_all, qbias, kbias, cosine, sine, wq, wk, wv)


def ep_perm(dyl, dz, dc):
    at = lambda yl, z, c: (yl * 4 + z) * 2 + c
    return [
        (at(yl, z, c), at(yl ^ dyl, (z + dz) % 4, c ^ dc)) for yl in range(2) for z in range(4) for c in range(2)
    ]


Z_UP, Z_DOWN, ACROSS, CORE = ep_perm(0, 1, 0), ep_perm(0, 3, 0), ep_perm(1, 0, 0), ep_perm(0, 0, 1)


def send(value, perm):
    return lax.ppermute(value, EP, perm)


def swap(value, axis):
    return lax.ppermute(value, axis, [(0, 1), (1, 0)])


def scatter_sum(own, oth):
    n, width = own.shape[1], own.shape[2]
    a, b = n * 3 // 8, n * 6 // 8
    wide = lambda v: v.astype(F32)
    none = lambda m: jnp.zeros((m, width), F32)
    t = wide(own) + wide(send(oth, CORE))
    far = t[7].astype(BF16)
    t1, t2, t3 = send(far[:a], ACROSS), send(far[a:b], Z_DOWN), send(far[b:], Z_UP)
    s3 = (t[3] + jnp.concatenate([wide(t1), none(n - a)], 0)).astype(BF16)
    s5 = (t[5] + jnp.concatenate([none(a), wide(t2), none(n - b)], 0)).astype(BF16)
    s6 = (t[6] + jnp.concatenate([none(b), wide(t3)], 0)).astype(BF16)
    u1, u2, u3 = send(s3, Z_DOWN), send(s6, Z_UP), send(s5, ACROSS)
    s1 = (t[1] + wide(u1) + wide(u3)).astype(BF16)
    s4 = (t[4] + wide(u2)).astype(BF16)
    v1, v2, v4 = send(s1, Z_DOWN), send(t[2].astype(BF16), Z_UP), send(s4, ACROSS)
    return t[0] + wide(v1) + wide(v2) + wide(v4)


def dense_sum(left, right, core):
    half = right.shape[1] // 2
    order = jnp.arange(D, dtype=jnp.int32).reshape(4, 2, 4, 40).transpose(2, 0, 1, 3).reshape(D)
    place = (jnp.arange(D, dtype=jnp.int32)[:, None] == order[None, :]).astype(BF16)
    left = jnp.dot(left, place, preferred_element_type=F32).astype(BF16)
    mine = jnp.where(core == 0, right[:, :half], right[:, half:])
    theirs = jnp.where(core == 0, right[:, half:], right[:, :half])
    out = lambda r: dot_tn(left, r).astype(BF16)
    both = (out(mine).astype(F32) + swap(out(theirs), "c").astype(F32)).astype(BF16)
    part = lax.psum_scatter(both, "z", scatter_dimension=0, tiled=True)
    parts = lax.all_to_all(part.reshape(8, 40, half), ("x", "yl"), split_axis=0, concat_axis=0, tiled=True)
    total = jnp.sum(parts.astype(F32), axis=0)
    first, second = total[:20], total[20:]
    keep = jnp.where(core == 0, first, second)
    got = swap(jnp.where(core == 0, second, first), "c")
    return jnp.concatenate([jnp.where(core == 0, keep, got), jnp.where(core == 0, got, keep)], axis=1)


def rotation(positions):
    half = HEAD_DIM // 2
    frequency = BASE ** (-(jnp.arange(half, dtype=F32) * 2.0) / HEAD_DIM)
    angles = positions.astype(F32)[:, None] * frequency[None, :]
    cosine, sine = jnp.cos(angles), jnp.sin(angles)
    return jnp.concatenate([cosine, cosine], axis=1), jnp.concatenate([-sine, sine], axis=1)


def mask_bias(query_pos, key_pos, query_doc, key_doc, starts, ends):
    visible = key_pos <= query_pos
    for j in range(starts.shape[0]):
        visible |= (query_pos >= starts[j]) & (query_pos < ends[j]) & (key_pos >= starts[j]) & (key_pos < ends[j])
    return jnp.where(visible & (query_doc == key_doc), 0.0, NEG_FILL).astype(F32)


def local(
    tokens, grad_out, doc_ids, piece_starts, piece_ends, routes, norm1_gain, norm2_gain, query_weight, key_weight, value_weight,
    output_weight, router_weight, shared_gate, shared_up, shared_down, expert_gate, expert_up, expert_down,
):
    core = lax.axis_index("c")
    rank = lax.axis_index(EP).astype(jnp.int32)
    group = lambda v: lax.all_gather(v, EP, axis=0, tiled=True)
    gain1, gain2 = norm1_gain[None, :], norm2_gain[None, :]
    wr = jnp.pad(router_weight, ((0, 0), (0, EXTRA - router_weight.shape[1])))
    own_pos = rank * T + jnp.arange(T, dtype=jnp.int32)
    cosine, sine = rotation(own_pos)
    keys_at = jnp.where(rank < 10, 0, 768).astype(jnp.int32)
    queries_at = jnp.where(rank < 6, 0, 768).astype(jnp.int32)
    at = jnp.stack([keys_at, queries_at])
    docs, starts, ends = doc_ids[0], piece_starts[0], piece_ends[0]
    own_doc = lax.dynamic_slice_in_dim(docs, rank * T, T)
    key_pos = keys_at + jnp.arange(KEYS, dtype=jnp.int32)
    query_pos = queries_at + jnp.arange(KEYS, dtype=jnp.int32)
    key_doc = lax.dynamic_slice_in_dim(docs, keys_at, KEYS)
    query_doc = lax.dynamic_slice_in_dim(docs, queries_at, KEYS)
    qbias = mask_bias(own_pos[:, None], key_pos[None, :], own_doc[:, None], key_doc[None, :], starts, ends)
    kbias = mask_bias(query_pos[None, :], own_pos[:, None], query_doc[None, :], own_doc[:, None], starts, ends)

    h1, q, kv, dyp, hot = project(
        tokens, gain1, query_weight, key_weight, value_weight, cosine, sine, routes, grad_out
    )
    kv_all = group(kv)
    dy_all = group(dyp)
    o, part, qp = attend(at, q, kv_all, qbias, output_weight)
    r, h2p, gates = gate(tokens, part, swap(part, "yh"), gain2, wr, hot)
    h2_all = group(h2p)
    q_all = group(qp)
    shared_out, shared_dh, sh, dsg, dsu = shared(h2p, grad_out, shared_gate, shared_up, shared_down)
    xb, dyg, eh, dgu, own, oth, yown, yoth = experts(
        rank[None], h2_all, dy_all, expert_gate, expert_up, expert_down
    )
    back = scatter_sum(own, oth)
    gu, down = expert_grads(xb, dyg, eh, dgu)
    gu = lax.psum_scatter(gu, "x", scatter_dimension=0, tiled=True)
    down = lax.psum_scatter(down, "x", scatter_dimension=0, tiled=True)
    back = jnp.concatenate([back[:, :D] + shared_dh, back[:, D:]], axis=1).astype(BF16)
    dr, da, dop, dlog, gain2_terms = middle(
        back, swap(back, "yh"), r, grad_out, h2p, gates, gain2, wr, output_weight, o
    )
    do_all = group(dop)
    mixed = (scatter_sum(yown, yoth) + shared_out).astype(BF16)
    output = (r + (mixed.astype(F32) + swap(mixed, "yh").astype(F32))).astype(BF16)

    put = lambda v, before, width: jnp.pad(v, ((0, 0), (before, width - before - v.shape[1])))
    one = jnp.ones((T, 1), BF16)
    left = jnp.concatenate([da, h2p[:, :D], grad_out, gain2_terms], axis=0)
    width = HW + 3 * FF + 64
    right = jnp.concatenate(
        [
            put(o.astype(BF16), 0, width),
            put(jnp.concatenate([dsg, dsu, jnp.zeros((T, FF), BF16), dlog[:, :63]], axis=1), HW, width),
            put(sh, HW + 2 * FF, width),
            put(one, width - 1, width),
        ],
        axis=0,
    )
    first = dense_sum(left, right, core)

    dqkv, dh1_part = attend_back(
        at, qp, kv, dop, kv_all, q_all, do_all, qbias, kbias, cosine, sine, query_weight, key_weight, value_weight
    )
    dh1 = dh1_part.astype(F32) + swap(dh1_part, "yh").astype(F32)
    x = tokens.astype(F32)
    inverse = lax.rsqrt(jnp.mean(x * x, axis=1, keepdims=True) + EPSILON)
    unit = x * inverse
    e1 = dh1 * gain1
    grad_tokens = dr + inverse * (e1 - unit * jnp.mean(e1 * unit, axis=1, keepdims=True))
    left = jnp.concatenate([h1, (dh1 * unit).astype(BF16)], axis=0)
    width = 3 * HW + 128
    right = jnp.concatenate([put(dqkv, 0, width), put(one, 3 * HW, width)], axis=0)
    second = dense_sum(left, right, core)

    o_at, s_at = 0, HW
    gu = gu.reshape(D // 4, E, 2, FF).astype(F32)
    return (
        output,
        grad_tokens,
        second[:, 3 * HW],
        first[:, HW + 3 * FF + 63],
        second[:, :HW],
        second[:, HW : 2 * HW],
        second[:, 2 * HW : 3 * HW],
        first[:, o_at : o_at + HW].T,
        first[:, HW + 3 * FF : HW + 3 * FF + 63],
        first[:, s_at : s_at + FF],
        first[:, s_at + FF : s_at + 2 * FF],
        first[:, s_at + 2 * FF : s_at + 3 * FF].T,
        gu[:, :, 0].transpose(1, 0, 2),
        gu[:, :, 1].transpose(1, 0, 2),
        down.reshape(D // 4, E, FF).astype(F32).transpose(1, 2, 0),
    )


def solution(mesh):
    fine = Mesh(mesh.devices.reshape(4, 2, 4, 2, 2), ("x", "yl", "z", "c", "yh"))
    rows64 = ("x", "yl", "z", "c")
    in_specs = (
        P(rows64, None),
        P(rows64, None),
        P("x", None),
        P("x", None),
        P("x", None),
        P(rows64, None),
        P(),
        P(),
        P(None, "yh"),
        P(None, "yh"),
        P(None, "yh"),
        P("yh", None),
        P(),
        P(None, "yh"),
        P(None, "yh"),
        P("yh", None),
        P(EP, None, "yh"),
        P(EP, None, "yh"),
        P(EP, "yh", None),
    )
    out_specs = (
        P(rows64, None),
        P(rows64, None),
        P(rows64),
        P(rows64),
        P(rows64, "yh"),
        P(rows64, "yh"),
        P(rows64, "yh"),
        P("yh", rows64),
        P(rows64, None),
        P(rows64, "yh"),
        P(rows64, "yh"),
        P("yh", rows64),
        P(EP, "x", "yh"),
        P(EP, "x", "yh"),
        P(EP, "yh", "x"),
    )
    return jax.shard_map(local, mesh=fine, in_specs=in_specs, out_specs=out_specs, check_vma=False)
```

time: 1080 us -> 554 us (0.51)
  local copies, waits for them, and re-layouts: 402 us -> 80.6 us
  waiting for transfers between devices: 443 us -> 301 us
  matrix products: 106 us -> 12.5 us
  Pallas kernels: 0 us -> 68.7 us
  other arithmetic: 53.9 us -> 26 us
    reduce_scatter x3 -> x4, waiting for transfers between devices: 312 us -> 121 us  [the longest x1 83.2 us: local(): gu = lax.psum_scatter(gu, 'x', scatter_dimension=0, tiled=True)]
    concatenate x4 -> x3, local copies, waits for them, and re-layouts: 116 us -> 1.22 us  [the longest x1 1.14 us: local(): jnp.concatenate([dsg, dsu, jnp.zeros((T, FF), BF16), dlog[:, :63]], axis=1)]
    dot_general x64 -> x6, matrix products: 106 us -> 12.5 us  [the longest x4 7.93 us: dot_tn(): lax.dot_general(a, b, (((0,), (0,)), ((), ())), preferred_element_type=F32)]
    ppermute x0 -> x28, waiting for transfers between devices: none -> 86.5 us  [the longest x20 49.6 us: send(): return lax.ppermute(value, EP, perm)]
    all_to_all x8 -> x2, waiting for transfers between devices: 92.7 us -> 8.33 us  [dense_sum(): lax.all_to_all(part.reshape(8, 40, half), ('x', 'yl'), split_axis=0, conc...]
    pallas_call x0 -> x8, Pallas kernels: none -> 68.7 us  [the longest x1 31.9 us: experts(): pl.pallas_call(experts_kernel, out_shape=(jax.ShapeDtypeStruct((E, n, D),...]
    reshape x21 -> x1, local copies, waits for them, and re-layouts: 50.7 us -> 0.09 us  [dense_sum(): jnp.arange(D, dtype=jnp.int32).reshape(4, 2, 4, 40).transpose(2, 0, 1, 3)]
    another operation x12 -> x0, local copies, waits for them, and re-layouts: 50.1 us -> none  [sum_packed(): lines = jnp.concatenate([b.reshape(size, -1) for b in blocks], axis=1)]
  transfers between devices with their start and end apart: 13 -> 39, of which waited for: 8 -> 25; matrix products, arithmetic and copies ran while one was open for 40% -> 18% of each run, Pallas kernels for 0% -> 6%
where the time goes in v1:
time: 554 us; the launch traced here: 546 us
  waiting for transfers between devices  301 us (54%)
  local copies, waits for them, and re-layouts  80.6 us (15%)
  Pallas kernels  68.7 us (12%)
  starting transfers between devices  42.6 us (8%)
  other arithmetic  26 us (5%)
  between operations  15 us (3%)
  matrix products  12.5 us (2%)
    all_gather x5, waiting for transfers between devices, local(): group = lambda v: lax.all_gather(v, EP, axis=0, tiled=True)  83.5 us
    reduce_scatter x1, waiting for transfers between devices, local(): gu = lax.psum_scatter(gu, 'x', scatter_dimension=0, tiled=True)  83.2 us
    ppermute x20, waiting for transfers between devices, send(): return lax.ppermute(value, EP, perm)  49.6 us
    unnamed x102, local copies, waits for them, and re-layouts  46.9 us
    ppermute x8, waiting for transfers between devices, swap(): return lax.ppermute(value, axis, [(0, 1), (1, 0)])  36.9 us
    pallas_call x1, Pallas kernels, experts(): pl.pallas_call(experts_kernel, out_shape=(jax.ShapeDtypeStruct((E, n, D),...  31.9 us
    reduce_scatter x2, waiting for transfers between devices, dense_sum(): part = lax.psum_scatter(both, 'z', scatter_dimension=0, tiled=True)  30.8 us
    ppermute x20, starting transfers between devices, send(): return lax.ppermute(value, EP, perm)  18.4 us
  transfers between devices with their start and end apart: 39, of which 25 were waited for; matrix products, arithmetic and copies ran while one was open for 18% of the time, Pallas kernels for 6%

profile of v1, /device:TPU:0, one launch (start us, length us, event | category | flops | bytes accessed | tf_op | source)
XLA Modules:
  0.0 546.1 jit_solution(18310689201550999906)
XLA Ops:
  29.8 30.6 %all-gather.6.cloned.1.call-done.kv_hbm = bf16[2048,1280]{1,0:T(8,128)(2,1)} async-done(((bf16[128,1280]{1,0:T(8,128)(2,1)}), bf16[2048,1280]{1,0:T(8,128)(2,1)}) %all-gather.6.cloned.1.call-update) | async-done | bytes 5242896 | tf_op jit(solution)/shard_map/all_gather | solution.py:569
  62.9 4.6 attend.1
  72.9 12.4 %collective-permute-done.b_ref = bf16[128,1280]{1,0:T(8,128)(2,1)} collective-permute-done((bf16[128,1280]{1,0:T(8,128)(2,1)S(1)}, bf16[128,1280]{1,0:T(8,128)(2,1)}, u32[]{:S(2)}, u32[]{:S(2)}) %collective-permute-start) | collective-permute-done | bytes 327712 | tf_op jit(solution)/shard_map/ppermute | solution.py:509
  89.5 7.7 %copy.45.wg_ref = bf16[4,1280,448]{2,1,0:T(8,128)(2,1)} copy(bf16[4,1280,448]{1,2,0:T(8,128)(2,1)} %param.35) | data formatting | bytes 9175040 | tf_op args[16]
  97.3 7.7 %copy.46.wu_ref = bf16[4,1280,448]{2,1,0:T(8,128)(2,1)} copy(bf16[4,1280,448]{1,2,0:T(8,128)(2,1)} %param.36) | data formatting | bytes 9175040 | tf_op args[17]
  108.1 40.8 %all-gather.8.cloned.1.call-done.h2_ref = bf16[2048,1408]{1,0:T(8,128)(2,1)} async-done(((bf16[128,1408]{1,0:T(8,128)(2,1)}), bf16[2048,1408]{1,0:T(8,128)(2,1)}) %all-gather.8.cloned.1.call-update) | async-done | bytes 5767184 | tf_op jit(solution)/shard_map/all_gather | solution.py:569
  148.9 31.9 %experts.1 = (bf16[4,256,1280]{2,1,0:T(8,128)(2,1)}, bf16[4,256,1280]{2,1,0:T(8,128)(2,1)}, bf16[4,256,896]{2,1,0:T(8,128)(2,1)}, bf16[4,256,896]{2,1,0:T(8,128)...) custom-call(s32[1]{0:T(128)} %bitcast.7.rank_ref, ...), custom_call_target="tpu_custom_call" | custom-call | flops 8220835840 | bytes 50000000 | tf_op jit(solution)/shard_map/experts/pallas_call | solution.py:318
  181.2 5.3 collective-permute-done.12
  193.4 5.3 collective-permute-done.15
  203.8 13.3 %collective-permute-done.14 = bf16[128,1408]{1,0:T(8,128)(2,1)S(1)} collective-permute-done((bf16[128,1408]{1,0:T(8,128)(2,1)S(1)}, bf16[128,1408]{1,0:T(8,128)(2,1)S(1)}, u32[]{:S(2)}, u32[]{:S(2)}) %collective-permute-start.14) | collective-permute-done | bytes 360480 | tf_op jit(solution)/shard_map/ppermute | solution.py:505
  240.3 6.1 %collective-permute-done.22.b_ref = bf16[128,1408]{1,0:T(8,128)(2,1)S(1)} collective-permute-done((bf16[128,1408]{1,0:T(8,128)(2,1)S(1)}, bf16[128,1408]{1,0:T(8,128)(2,1)S(1)}, u32[]{:S(2)}, u32[]{:S(2)}) %collective-permute-start.22) | collective-permute-done | bytes 360480 | tf_op jit(solution)/shard_map/ppermute | solution.py:509
  261.3 4.9 collective-permute-done.26
  269.5 9.8 %expert_grads.1 = (bf16[1280,3584]{1,0:T(8,128)(2,1)}, bf16[1280,1792]{1,0:T(8,128)(2,1)}) custom-call(bf16[4,256,1280]{2,1,0:T(8,128)(2,1)} %get-tuple-element.75.x_ref, bf16[4,256,1280]{2,1,0:T(8,128)(2,1)} %get-tuple-element.76.dy_ref, bf16[4,256,896]{2,1,0:T(8,128)(2,1)} %get-tuple-element.77.eh_ref, bf16[4,256,896]{2,1,0:T(8,128)(2,1)} %get-tuple-element.78.dgu_ref), custom_call_target="tpu_custom_call" | custom-call | flops 3523215360 | bytes 30000000 | tf_op jit(solution)/shard_map/expert_grads/pallas_call | solution.py:366
  279.6 8.9 %all-gather.14.cloned.1.call-done.do_hbm = bf16[2048,768]{1,0:T(8,128)(2,1)} async-done(((bf16[128,768]{1,0:T(8,128)(2,1)}), bf16[2048,768]{1,0:T(8,128)(2,1)}) %all-gather.14.cloned.1.call-update) | async-done | bytes 3145744 | tf_op jit(solution)/shard_map/all_gather | solution.py:569
  288.5 12.0 %attend_back.1 = (bf16[128,1920]{1,0:T(8,128)(2,1)S(1)}, bf16[128,1280]{1,0:T(8,128)(2,1)S(1)}) custom-call(s32[2]{0:T(128)S(1)} %pad_add_fusion.at_ref, bf16[128,768]{1,0:T(8,128)(2,1)} %get-tuple-element.64.qp_ref, bf16[128,1280]{1,0:T(8,128)(2,1)} %get-tuple-element.49.kv_ref, bf16[128,768]{1,0:T(8,128)(2,1)} %get-tuple-element.65.dop_ref, ...), custom_call_target="tpu_custom_call" | custom-call | flops 2306867200 | bytes 20000000 | tf_op jit(solution)/shard_map/attend_back/pallas_call | solution.py:477
  303.5 8.5 %collective-permute-done.23 = bf16[128,1280]{1,0:T(8,128)(2,1)S(1)} collective-permute-done((bf16[128,1280]{1,0:T(8,128)(2,1)S(1)}, bf16[128,1280]{1,0:T(8,128)(2,1)S(1)}, u32[]{:S(2)}, u32[]{:S(2)}) %collective-permute-start.23) | collective-permute-done | bytes 327712 | tf_op jit(solution)/shard_map/ppermute | solution.py:509
  316.2 4.9 collective-permute-done.24
  324.4 5.0 collective-permute-done.1
  342.1 4.6 collective-permute-done.3
  347.5 4.4 collective-permute-done.9
  353.8 4.8 all-to-all-start.1
  358.6 3.5 collective-permute-done.10
  363.4 4.3 collective-permute-start.11
  367.7 8.3 %all-to-all-done.1 = bf16[8,40,1024]{2,1,0:T(8,128)(2,1)S(1)} async-done(((bf16[8,40,1024]{2,1,0:T(8,128)(2,1)}), bf16[8,40,1024]{2,1,0:T(8,128)(2,1)S(1)}, u32[]{:S(2)}, u32[]{:S(2)}) %all-to-all-start.1) | async-done | bytes 655392 | tf_op jit(solution)/shard_map/all_to_all | solution.py:540
  377.0 6.9 %reduce-scatter.11.cloned.1.call-done = bf16[320,1792]{1,0:T(8,128)(2,1)} async-done(((bf16[1280,1792]{1,0:T(8,128)(2,1)}), bf16[320,1792]{1,0:T(8,128)(2,1)}) %reduce-scatter.11.cloned.1.call-update) | async-done | bytes 1146896 | tf_op jit(solution)/shard_map/reduce_scatter | solution.py:602
  384.0 3.8 reshape.246
  390.1 30.8 %reduce-scatter.5.cloned.1.call-done = bf16[320,1024]{1,0:T(8,128)(2,1)} async-done(((bf16[1280,1024]{1,0:T(8,128)(2,1)}), bf16[320,1024]{1,0:T(8,128)(2,1)}) %reduce-scatter.5.cloned.1.call-update) | async-done | bytes 655376 | tf_op jit(solution)/shard_map/reduce_scatter | solution.py:539
  420.9 5.2 all-to-all-start
  428.8 83.2 %reduce-scatter.9.cloned.1.call-done = bf16[320,3584]{1,0:T(8,128)(2,1)} async-done(((bf16[1280,3584]{1,0:T(8,128)(2,1)}), bf16[320,3584]{1,0:T(8,128)(2,1)}) %reduce-scatter.9.cloned.1.call-update) | async-done | bytes 2293776 | tf_op jit(solution)/shard_map/reduce_scatter | solution.py:601
  512.1 7.9 %reshape.245 = f32[320,4,2,448]{3,2,1,0:T(2,128)} reshape(bf16[320,3584]{1,0:T(8,128)(2,1)} %reduce-scatter.9.cloned.1.call-done) | data formatting | bytes 6881280 | tf_op jit(solution)/shard_map/convert_element_type | solution.py:641
  520.5 10.9 %fusion.104 = (f32[320,4,1,448]{3,2,1,0:T(1,128)}, f32[320,4,1,448]{3,2,1,0:T(1,128)S(1)}) fusion(f32[320,4,2,448]{3,2,1,0:T(2,128)} %reshape.245), kind=kLoop, calls=%fused_computation.188 | loop fusion | bytes 9175040 | tf_op jit(solution)/shard_map/slice | solution.py:656
  531.5 4.1 copy.57
  (244 shorter events, 128.5 us)
Async XLA Ops:
  7.2 53.2 %all-gather.6.cloned.1.call-start = ((), (), s32[]{:S(2)}) async-start(), calls=%async_computation.6 | async-start | bytes 5570560 | tf_op jit(solution)/shard_map/all_gather | solution.py:569
  18.3 89.8 %all-gather.10.cloned.1.call-start = ((), (), s32[]{:S(2)}) async-start(), calls=%async_computation.8 | async-start | bytes 6127616 | tf_op jit(solution)/shard_map/all_gather | solution.py:569
  19.0 129.9 %all-gather.8.cloned.1.call-start = ((), (), s32[]{:S(2)}) async-start(), calls=%async_computation.7 | async-start | bytes 6127616 | tf_op jit(solution)/shard_map/all_gather | solution.py:569
  68.2 17.1 %collective-permute-start = (bf16[128,1280]{1,0:T(8,128)(2,1)S(1)}, bf16[128,1280]{1,0:T(8,128)(2,1)}, u32[]{:S(2)}, u32[]{:S(2)}) collective-permute-start(bf16[128,1280]{1,0:T(8,128)(2,1)S(1)} %get-tuple-element.50.a_ref), channel_id=1, source_target_pairs={{0,1},{1,0},{2,3},{3,2},{4,5},{5,4},{6,7},{7,6},{8,9},{9,8},{10,11... | collective-permute-start | bytes 983048 | tf_op jit(solution)/shard_map/ppermute | solution.py:509
  89.3 190.4 %all-gather.12.cloned.1.call-start = ((), (), s32[]{:S(2)}) async-start(), calls=%async_computation.9 | async-start | bytes 3342336 | tf_op jit(solution)/shard_map/all_gather | solution.py:569
  181.1 107.4 %all-gather.14.cloned.1.call-start = ((), (), s32[]{:S(2)}) async-start(), calls=%async_computation.10 | async-start | bytes 3342336 | tf_op jit(solution)/shard_map/all_gather | solution.py:569
  190.0 8.6 %collective-permute-start.15 = (bf16[48,1408]{1,0:T(8,128)(2,1)S(1)}, bf16[48,1408]{1,0:T(8,128)(2,1)S(1)}, u32[]{:S(2)}, u32[]{:S(2)}) collective-permute-start(bf16[48,1408]{1,0:T(8,128)(2,1)S(1)} %get-tuple-element.106), channel_id=1, source_target_pairs={{0,12},{2,14},{4,0},{6,2},{8,4},{10,6},{12,8},{14,10},{16,28},{18,... | collective-permute-start | bytes 405512 | tf_op jit(solution)/shard_map/ppermute | solution.py:505
  192.1 6.8 %collective-permute-start.13 = (bf16[48,1408]{1,0:T(8,128)(2,1)S(1)}, bf16[48,1408]{1,0:T(8,128)(2,1)S(1)}, u32[]{:S(2)}, u32[]{:S(2)}) collective-permute-start(bf16[48,1408]{1,0:T(8,128)(2,1)S(1)} %get-tuple-element.105), channel_id=1, source_target_pairs={{0,16},{2,18},{4,20},{6,22},{8,24},{10,26},{12,28},{14,30},{16,0},... | collective-permute-start | bytes 405512 | tf_op jit(solution)/shard_map/ppermute | solution.py:505
  199.1 18.0 %collective-permute-start.14 = (bf16[128,1408]{1,0:T(8,128)(2,1)S(1)}, bf16[128,1408]{1,0:T(8,128)(2,1)S(1)}, u32[]{:S(2)}, u32[]{:S(2)}) collective-permute-start(bf16[128,1408]{1,0:T(8,128)(2,1)S(1)} %get-tuple-element.91), channel_id=1, source_target_pairs={{0,12},{2,14},{4,0},{6,2},{8,4},{10,6},{12,8},{14,10},{16,28},{18,... | collective-permute-start | bytes 1081352 | tf_op jit(solution)/shard_map/ppermute | solution.py:505
  201.8 17.5 %collective-permute-start.16 = (bf16[128,1408]{1,0:T(8,128)(2,1)S(1)}, bf16[128,1408]{1,0:T(8,128)(2,1)S(1)}, u32[]{:S(2)}, u32[]{:S(2)}) collective-permute-start(bf16[128,1408]{1,0:T(8,128)(2,1)S(1)} %get-tuple-element.92), channel_id=1, source_target_pairs={{0,16},{2,18},{4,20},{6,22},{8,24},{10,26},{12,28},{14,30},{16,0},... | collective-permute-start | bytes 1081352 | tf_op jit(solution)/shard_map/ppermute | solution.py:505
  202.6 16.7 %collective-permute-start.20 = (bf16[128,1408]{1,0:T(8,128)(2,1)S(1)}, bf16[128,1408]{1,0:T(8,128)(2,1)S(1)}, u32[]{:S(2)}, u32[]{:S(2)}) collective-permute-start(bf16[128,1408]{1,0:T(8,128)(2,1)S(1)} %get-tuple-element.93), channel_id=1, source_target_pairs={{0,4},{2,6},{4,8},{6,10},{8,12},{10,14},{12,0},{14,2},{16,20},{18,... | collective-permute-start | bytes 1081352 | tf_op jit(solution)/shard_map/ppermute | solution.py:505
  203.3 32.0 %collective-permute-start.18 = (bf16[128,1408]{1,0:T(8,128)(2,1)}, bf16[128,1408]{1,0:T(8,128)(2,1)}, u32[]{:S(2)}, u32[]{:S(2)}) collective-permute-start(bf16[128,1408]{1,0:T(8,128)(2,1)} %slice_bitcast_fusion.12), channel_id=1, source_target_pairs={{0,4},{2,6},{4,8},{6,10},{8,12},{10,14},{12,0},{14,2},{16,20},{18,... | collective-permute-start | bytes 1081352 | tf_op jit(solution)/shard_map/ppermute | solution.py:505
  220.4 14.9 %collective-permute-start.17 = (bf16[128,1408]{1,0:T(8,128)(2,1)}, bf16[128,1408]{1,0:T(8,128)(2,1)}, u32[]{:S(2)}, u32[]{:S(2)}) collective-permute-start(bf16[128,1408]{1,0:T(8,128)(2,1)} %get-tuple-element.89), channel_id=1, source_target_pairs={{0,12},{2,14},{4,0},{6,2},{8,4},{10,6},{12,8},{14,10},{16,28},{18,... | collective-permute-start | bytes 1081352 | tf_op jit(solution)/shard_map/ppermute | solution.py:505
  223.0 12.3 %collective-permute-start.21 = (bf16[128,1408]{1,0:T(8,128)(2,1)}, bf16[128,1408]{1,0:T(8,128)(2,1)}, u32[]{:S(2)}, u32[]{:S(2)}) collective-permute-start(bf16[128,1408]{1,0:T(8,128)(2,1)} %get-tuple-element.90), channel_id=1, source_target_pairs={{0,16},{2,18},{4,20},{6,22},{8,24},{10,26},{12,28},{14,30},{16,0},... | collective-permute-start | bytes 1081352 | tf_op jit(solution)/shard_map/ppermute | solution.py:505
  237.4 9.0 %collective-permute-start.22 = (bf16[128,1408]{1,0:T(8,128)(2,1)S(1)}, bf16[128,1408]{1,0:T(8,128)(2,1)S(1)}, u32[]{:S(2)}, u32[]{:S(2)}) collective-permute-start(bf16[128,1408]{1,0:T(8,128)(2,1)S(1)} %pad_maximum_fusion.a_ref), channel_id=1, source_target_pairs={{0,1},{1,0},{2,3},{3,2},{4,5},{5,4},{6,7},{7,6},{8,9},{9,8},{10,11... | collective-permute-start | bytes 1081352 | tf_op jit(solution)/shard_map/ppermute | solution.py:509
  252.3 101.5 %reduce-scatter.7.cloned.1.call-start = ((), (), s32[]{:S(2)}) async-start(), calls=%async_computation.12 | async-start | bytes 3276800 | tf_op jit(solution)/shard_map/reduce_scatter | solution.py:539
  269.3 114.7 %reduce-scatter.11.cloned.1.call-start = ((), (), s32[]{:S(2)}) async-start(), calls=%async_computation.14 | async-start | bytes 5734400 | tf_op jit(solution)/shard_map/reduce_scatter | solution.py:602
  279.4 141.5 %reduce-scatter.5.cloned.1.call-start = ((), (), s32[]{:S(2)}) async-start(), calls=%async_computation.11 | async-start | bytes 3276800 | tf_op jit(solution)/shard_map/reduce_scatter | solution.py:539
  300.6 11.4 %collective-permute-start.23 = (bf16[128,1280]{1,0:T(8,128)(2,1)S(1)}, bf16[128,1280]{1,0:T(8,128)(2,1)S(1)}, u32[]{:S(2)}, u32[]{:S(2)}) collective-permute-start(bf16[128,1280]{1,0:T(8,128)(2,1)S(1)} %get-tuple-element.66), channel_id=1, source_target_pairs={{0,1},{1,0},{2,3},{3,2},{4,5},{5,4},{6,7},{7,6},{8,9},{9,8},{10,11... | collective-permute-start | bytes 983048 | tf_op jit(solution)/shard_map/ppermute | solution.py:509
  323.5 188.6 %reduce-scatter.9.cloned.1.call-start = ((), (), s32[]{:S(2)}) async-start(), calls=%async_computation.13 | async-start | bytes 11468800 | tf_op jit(solution)/shard_map/reduce_scatter | solution.py:601
  332.0 6.4 %collective-permute-start.2 = (bf16[48,1280]{1,0:T(8,128)(2,1)S(1)}, bf16[48,1280]{1,0:T(8,128)(2,1)S(1)}, u32[]{:S(2)}, u32[]{:S(2)}) collective-permute-start(bf16[48,1280]{1,0:T(8,128)(2,1)S(1)} %get-tuple-element.107), channel_id=1, source_target_pairs={{0,16},{2,18},{4,20},{6,22},{8,24},{10,26},{12,28},{14,30},{16,0},... | collective-permute-start | bytes 368648 | tf_op jit(solution)/shard_map/ppermute | solution.py:505
  338.6 8.1 %collective-permute-start.3 = (bf16[128,1280]{1,0:T(8,128)(2,1)S(1)}, bf16[128,1280]{1,0:T(8,128)(2,1)S(1)}, u32[]{:S(2)}, u32[]{:S(2)}) collective-permute-start(bf16[128,1280]{1,0:T(8,128)(2,1)S(1)} %get-tuple-element.100), channel_id=1, source_target_pairs={{0,12},{2,14},{4,0},{6,2},{8,4},{10,6},{12,8},{14,10},{16,28},{18,... | collective-permute-start | bytes 983048 | tf_op jit(solution)/shard_map/ppermute | solution.py:505
  338.9 8.6 %collective-permute-start.5 = (bf16[128,1280]{1,0:T(8,128)(2,1)S(1)}, bf16[128,1280]{1,0:T(8,128)(2,1)S(1)}, u32[]{:S(2)}, u32[]{:S(2)}) collective-permute-start(bf16[128,1280]{1,0:T(8,128)(2,1)S(1)} %get-tuple-element.101), channel_id=1, source_target_pairs={{0,16},{2,18},{4,20},{6,22},{8,24},{10,26},{12,28},{14,30},{16,0},... | collective-permute-start | bytes 983048 | tf_op jit(solution)/shard_map/ppermute | solution.py:505
  340.1 11.9 %collective-permute-start.9 = (bf16[128,1280]{1,0:T(8,128)(2,1)S(1)}, bf16[128,1280]{1,0:T(8,128)(2,1)S(1)}, u32[]{:S(2)}, u32[]{:S(2)}) collective-permute-start(bf16[128,1280]{1,0:T(8,128)(2,1)S(1)} %get-tuple-element.102), channel_id=1, source_target_pairs={{0,4},{2,6},{4,8},{6,10},{8,12},{10,14},{12,0},{14,2},{16,20},{18,... | collective-permute-start | bytes 983048 | tf_op jit(solution)/shard_map/ppermute | solution.py:505
  342.0 16.6 %collective-permute-start.7 = (bf16[128,1280]{1,0:T(8,128)(2,1)S(1)}, bf16[128,1280]{1,0:T(8,128)(2,1)S(1)}, u32[]{:S(2)}, u32[]{:S(2)}) collective-permute-start(bf16[128,1280]{1,0:T(8,128)(2,1)S(1)} %slice_bitcast_fusion.13), channel_id=1, source_target_pairs={{0,4},{2,6},{4,8},{6,10},{8,12},{10,14},{12,0},{14,2},{16,20},{18,... | collective-permute-start | bytes 983048 | tf_op jit(solution)/shard_map/ppermute | solution.py:505
  352.9 9.2 %collective-permute-start.10 = (bf16[128,1280]{1,0:T(8,128)(2,1)}, bf16[128,1280]{1,0:T(8,128)(2,1)S(1)}, u32[]{:S(2)}, u32[]{:S(2)}) collective-permute-start(bf16[128,1280]{1,0:T(8,128)(2,1)} %get-tuple-element.99), channel_id=1, source_target_pairs={{0,16},{2,18},{4,20},{6,22},{8,24},{10,26},{12,28},{14,30},{16,0},... | collective-permute-start | bytes 983048 | tf_op jit(solution)/shard_map/ppermute | solution.py:505
  353.8 8.3 %collective-permute-start.6 = (bf16[128,1280]{1,0:T(8,128)(2,1)}, bf16[128,1280]{1,0:T(8,128)(2,1)S(1)}, u32[]{:S(2)}, u32[]{:S(2)}) collective-permute-start(bf16[128,1280]{1,0:T(8,128)(2,1)} %get-tuple-element.98), channel_id=1, source_target_pairs={{0,12},{2,14},{4,0},{6,2},{8,4},{10,6},{12,8},{14,10},{16,28},{18,... | collective-permute-start | bytes 983048 | tf_op jit(solution)/shard_map/ppermute | solution.py:505
  353.8 22.2 %all-to-all-start.1 = ((bf16[8,40,1024]{2,1,0:T(8,128)(2,1)}), bf16[8,40,1024]{2,1,0:T(8,128)(2,1)S(1)}, u32[]{:S(2)}, u32[]{:S(2)}) async-start(bf16[8,40,1024]{2,1,0:T(8,128)(2,1)} %bitcast.137), calls=%async_computation.3 | async-start | bytes 1310720 | tf_op jit(solution)/shard_map/all_to_all | solution.py:540
  363.4 12.8 %collective-permute-start.11 = (bf16[128,1280]{1,0:T(8,128)(2,1)S(1)}, bf16[128,1280]{1,0:T(8,128)(2,1)S(1)}, u32[]{:S(2)}, u32[]{:S(2)}) collective-permute-start(bf16[128,1280]{1,0:T(8,128)(2,1)S(1)} %fusion.72), channel_id=1, source_target_pairs={{0,1},{1,0},{2,3},{3,2},{4,5},{5,4},{6,7},{7,6},{8,9},{9,8},{10,11... | collective-permute-start | bytes 983048 | tf_op jit(solution)/shard_map/ppermute | solution.py:509
  376.1 50.0 %collective-permute-start.27 = (f32[20,1024]{1,0:T(8,128)S(1)}, f32[20,1024]{1,0:T(8,128)S(1)}, u32[]{:S(2)}, u32[]{:S(2)}) collective-permute-start(f32[20,1024]{1,0:T(8,128)S(1)} %slice_select_fusion.1), channel_id=1, source_target_pairs={{0,2},{2,0},{1,3},{3,1},{4,6},{6,4},{5,7},{7,5},{8,10},{10,8},{9,1... | collective-permute-start | bytes 245768 | tf_op jit(solution)/shard_map/ppermute | solution.py:509
  420.9 99.1 %all-to-all-start = ((bf16[8,40,1024]{2,1,0:T(8,128)(2,1)}), bf16[8,40,1024]{2,1,0:T(8,128)(2,1)S(1)}, u32[]{:S(2)}, u32[]{:S(2)}) async-start(bf16[8,40,1024]{2,1,0:T(8,128)(2,1)} %bitcast.138), calls=%async_computation.1 | async-start | bytes 1310720 | tf_op jit(solution)/shard_map/all_to_all | solution.py:540
  520.1 17.7 %collective-permute-start.25 = (f32[20,1024]{1,0:T(8,128)S(1)}, f32[20,1024]{1,0:T(8,128)S(1)}, u32[]{:S(2)}, u32[]{:S(2)}) collective-permute-start(f32[20,1024]{1,0:T(8,128)S(1)} %slice_select_fusion.3), channel_id=1, source_target_pairs={{0,2},{2,0},{1,3},{3,1},{4,6},{6,4},{5,7},{7,5},{8,10},{10,8},{9,1... | collective-permute-start | bytes 245768 | tf_op jit(solution)/shard_map/ppermute | solution.py:509
  (54 other events, 458.3 us)
Sparse Core Ops, SparseCore 0:
  18.4 41.9 all-gather.5
  62.7 45.3 all-gather.9
  109.8 39.0 all-gather.7
  181.3 41.0 all-gather.11
  252.5 36.0 all-gather.13
  290.8 34.0 reduce-scatter.6
  327.3 56.5 reduce-scatter.10
  387.0 33.8 reduce-scatter.4
  423.4 88.6 reduce-scatter.8
